TPU v7x, 32 devices: a whole 2x2x4 slice. The times are simulated.
32 devices in a mesh: section: 4 (over x, core), dp: 8 (over z, y).
Axes of the slice: x: 2, y: 2, z: 4, core: 2. Of those that a mesh axis runs over, the one named last changes fastest.
Arguments:
- section_ins: bfloat16 [4, 8192, 768], P('section', 'dp'), may hold values from -6 to 6
- segments: int32 [16, 512], P('dp'), may hold values from 0 to 3, never falling along the last dimension, each value on 1 to 256 neighbouring positions
- buckets: int32 [2, 1023], replicated, may hold values from 0 to 31
- section_mats: bfloat16 [4, 3, 768, 3072], P('section'), may hold values from -3 to 3
- gains: float32 [7, 768], replicated, may hold values from 0.1 to 1.9
- tables: float32 [2, 32, 12], replicated, may hold values from -4 to 4
Outputs:
- section_outs: float32 [4, 8192, 768], P('section', 'dp')
- mats_grad: float32 [4, 3, 768, 3072], P('section', None, 'dp')
- gains_grad: float32 [7, 768], replicated
- tables_grad: float32 [2, 32, 12], replicated
All inputs are finite; a program needn't handle non-finite values.
Results may differ from a plain program's by a relative error of at most 0.025.
Values may be sent and summed in bfloat16 or wider, within the bound.
No kernel may reach another device: no remote copies, remote signals or barrier semaphores. Data moves between devices by JAX's collectives and lax.ppermute only.
A program may use at most 384 MiB of HBM per device.

v0:
```python
import jax
import jax.numpy as jnp
from jax import lax
from jax.sharding import PartitionSpec as P

H = 12
MICRO = 2


epsilon = 1e-06
negative_fill = -1000000000.0
highest = lax.Precision.HIGHEST
gelu_coef = 0.7978845608028654


def passed_along(value, axis, steps):
    count = lax.axis_size(axis)
    leading, last = (max(0, -steps), min(count, count - steps))
    return lax.ppermute(value, axis, [(source, source + steps) for source in range(leading, last)])


def for_sending(value):

    def short(part):
        return part.astype(jnp.bfloat16) if part.dtype == jnp.float32 else part

    return jax.tree.map(short, value)


def rms_forward(stream, gain):
    scale = lax.rsqrt(jnp.mean(stream * stream, axis=-1, keepdims=True) + epsilon)
    return (stream * scale * gain, scale)


def rms_backward(stream, scale, gain, upstream):
    gain_grad = jnp.sum(upstream * stream * scale, axis=0)
    inner = jnp.mean(upstream * gain * stream, axis=-1, keepdims=True)
    return (scale * gain * upstream - stream * (scale * scale * scale) * inner, gain_grad)


def gelu_slope(upward):
    tangent = jnp.tanh(gelu_coef * (upward + 0.044715 * upward * upward * upward))
    return 0.5 * (1.0 + tangent) + 0.5 * upward * (1.0 - tangent * tangent) * gelu_coef * (
        1.0 + 3.0 * 0.044715 * upward * upward
    )


def only_on(flag, compute, *operands):

    def blank(*inner):
        return jax.tree.map(jnp.zeros_like, compute(*inner))

    return lax.cond(flag, compute, blank, *operands)


def spread_diagonals(per_head, length):
    heads = per_head.shape[0]
    padded = jnp.concatenate([per_head, jnp.zeros((heads, 1), jnp.float32)], axis=1)
    tiled = jnp.tile(padded, (1, length))[:, : length * (2 * length - 1)]
    return tiled.reshape(heads, length, 2 * length - 1)[:, :, length - 1 :]


def sum_diagonals(grid, length):
    heads = grid.shape[0]
    shifted = jnp.concatenate([jnp.zeros((heads, length, length - 1), jnp.float32), grid], axis=2)
    shifted = shifted.reshape(heads, length * (2 * length - 1))
    shifted = jnp.concatenate([shifted, jnp.zeros((heads, length), jnp.float32)], axis=1)
    shifted = shifted.reshape(heads, length, 2 * length)
    return jnp.sum(shifted[:, :, : 2 * length - 1], axis=1)


def distance_bias(table, bucket_row, length):
    onehot = (bucket_row[:, None] == jnp.arange(table.shape[0], dtype=jnp.int32)[None, :]).astype(
        jnp.float32
    )
    per_distance = jnp.dot(onehot, table, precision=highest)
    return (spread_diagonals(per_distance.T, length), onehot)


def row_mask(row_segs, causal):
    length = row_segs.shape[0]
    same = row_segs[:, None] == row_segs[None, :]
    earlier = jnp.arange(length)[None, :] <= jnp.arange(length)[:, None]
    return same & (earlier | jnp.logical_not(causal))


def attend_rows(query, keys, values, segs, bias, causal):
    rows, length = segs.shape
    width = query.shape[1]
    head_dim = width // H

    def one_row(items):
        row_query, row_keys, row_values, row_segs = items
        query_heads = row_query.reshape(length, H, head_dim)
        key_heads = row_keys.reshape(length, H, head_dim)
        value_heads = row_values.reshape(length, H, head_dim)
        scores = (
            jnp.einsum("ihd,jhd->hij", query_heads, key_heads, preferred_element_type=jnp.float32)
            + bias
        )
        scores = jnp.where(row_mask(row_segs, causal)[None], scores, negative_fill)
        top = jnp.max(scores, axis=-1, keepdims=True)
        exponent = jnp.exp(scores - top)
        total = jnp.sum(exponent, axis=-1, keepdims=True)
        weights = (exponent / total).astype(jnp.bfloat16)
        mixed = jnp.einsum("hij,jhd->ihd", weights, value_heads, preferred_element_type=jnp.float32)
        return (mixed.reshape(length, width), (top + jnp.log(total))[:, :, 0])

    mixed, logsum = lax.map(
        one_row,
        (
            query.reshape(rows, length, width),
            keys.reshape(rows, length, width),
            values.reshape(rows, length, width),
            segs,
        ),
    )
    return (mixed.reshape(rows * length, width), logsum)


def attend_back(query, keys, values, segs, bias, causal, logsum, grad_mixed, with_bias):
    rows, length = segs.shape
    width = query.shape[1]
    head_dim = width // H

    def one_row(carry, items):
        row_query, row_keys, row_values, row_segs, row_logsum, row_grad = items
        query_heads = row_query.reshape(length, H, head_dim)
        key_heads = row_keys.reshape(length, H, head_dim)
        value_heads = row_values.reshape(length, H, head_dim)
        grad_heads = row_grad.reshape(length, H, head_dim)
        scores = (
            jnp.einsum("ihd,jhd->hij", query_heads, key_heads, preferred_element_type=jnp.float32)
            + bias
        )
        scores = jnp.where(row_mask(row_segs, causal)[None], scores, negative_fill)
        weights = jnp.exp(scores - row_logsum[:, :, None])
        grad_weights = jnp.einsum(
            "ihd,jhd->hij", grad_heads, value_heads, preferred_element_type=jnp.float32
        )
        inner = jnp.sum(weights * grad_weights, axis=-1, keepdims=True)
        grad_scores = (weights * (grad_weights - inner)).astype(jnp.bfloat16)
        grad_values = jnp.einsum(
            "hij,ihd->jhd",
            weights.astype(jnp.bfloat16),
            grad_heads,
            preferred_element_type=jnp.float32,
        )
        grad_query = jnp.einsum(
            "hij,jhd->ihd", grad_scores, key_heads, preferred_element_type=jnp.float32
        )
        grad_keys = jnp.einsum(
            "hij,ihd->jhd", grad_scores, query_heads, preferred_element_type=jnp.float32
        )
        if with_bias:
            carry = carry + grad_scores.astype(jnp.float32)
        return (
            carry,
            (
                grad_query.reshape(length, width),
                grad_keys.reshape(length, width),
                grad_values.reshape(length, width),
            ),
        )

    if with_bias:
        start_sum = jnp.zeros((H, length, length), jnp.float32)
    else:
        start_sum = jnp.zeros((H, 1), jnp.float32)
    items = (
        query.reshape(rows, length, width),
        keys.reshape(rows, length, width),
        values.reshape(rows, length, width),
        segs,
        logsum,
        grad_mixed.reshape(rows, length, width),
    )
    summed, (grad_query, grad_keys, grad_values) = lax.scan(one_row, start_sum, items)
    if with_bias:
        diagonal = sum_diagonals(summed, length)
    else:
        diagonal = jnp.zeros((H, 2 * length - 1), jnp.float32)
    total_rows = rows * length
    return (
        grad_query.reshape(total_rows, width),
        grad_keys.reshape(total_rows, width),
        grad_values.reshape(total_rows, width),
        diagonal,
    )


def self_forward(stream, gain, weight, bias, segs, causal):
    width = stream.shape[1]
    normed, scale = rms_forward(stream, gain)
    normed = normed.astype(jnp.bfloat16)
    projected = jnp.dot(normed, weight[:, : 3 * width], preferred_element_type=jnp.float32).astype(
        jnp.bfloat16
    )
    mixed, logsum = attend_rows(
        projected[:, :width],
        projected[:, width : 2 * width],
        projected[:, 2 * width :],
        segs,
        bias,
        causal,
    )
    mixed = mixed.astype(jnp.bfloat16)
    result = stream + jnp.dot(mixed, weight[:, 3 * width :], preferred_element_type=jnp.float32)
    return (result, (normed, scale, projected, logsum, mixed))


def self_backward(stream, gain, weight, bias, segs, causal, kept, upstream):
    width = stream.shape[1]
    normed, scale, projected, logsum, mixed = kept
    grad_out = upstream.astype(jnp.bfloat16)
    grad_mixed = jnp.dot(
        grad_out, weight[:, 3 * width :].T, preferred_element_type=jnp.float32
    ).astype(jnp.bfloat16)
    grad_query, grad_keys, grad_values, diagonal = attend_back(
        projected[:, :width],
        projected[:, width : 2 * width],
        projected[:, 2 * width :],
        segs,
        bias,
        causal,
        logsum,
        grad_mixed,
        True,
    )
    grad_projected = jnp.concatenate([grad_query, grad_keys, grad_values], axis=1).astype(
        jnp.bfloat16
    )
    grad_normed = jnp.dot(
        grad_projected, weight[:, : 3 * width].T, preferred_element_type=jnp.float32
    )
    grad_stream, gain_grad = rms_backward(stream, scale, gain, grad_normed)
    return (upstream + grad_stream, gain_grad, diagonal, (grad_out, grad_projected))


def self_weights(kept, grads):
    grad_out, grad_projected = grads
    first = jnp.einsum("td,te->de", kept[0], grad_projected, preferred_element_type=jnp.float32)
    second = jnp.einsum("td,te->de", kept[4], grad_out, preferred_element_type=jnp.float32)
    return jnp.concatenate([first, second], axis=1)


def cross_forward(stream, memory, gain, weight, segs):
    width = stream.shape[1]
    normed, scale = rms_forward(stream, gain)
    normed = normed.astype(jnp.bfloat16)
    query = jnp.dot(normed, weight[:, :width], preferred_element_type=jnp.float32).astype(
        jnp.bfloat16
    )
    keyval = jnp.dot(
        memory, weight[:, width : 3 * width], preferred_element_type=jnp.float32
    ).astype(jnp.bfloat16)
    mixed, logsum = attend_rows(query, keyval[:, :width], keyval[:, width:], segs, 0.0, False)
    mixed = mixed.astype(jnp.bfloat16)
    result = stream + jnp.dot(mixed, weight[:, 3 * width :], preferred_element_type=jnp.float32)
    return (result, (normed, scale, query, keyval, logsum, mixed))


def cross_backward(stream, gain, weight, segs, kept, upstream):
    width = stream.shape[1]
    normed, scale, query, keyval, logsum, mixed = kept
    grad_out = upstream.astype(jnp.bfloat16)
    grad_mixed = jnp.dot(
        grad_out, weight[:, 3 * width :].T, preferred_element_type=jnp.float32
    ).astype(jnp.bfloat16)
    grad_query, grad_keys, grad_values, unused_sum = attend_back(
        query, keyval[:, :width], keyval[:, width:], segs, 0.0, False, logsum, grad_mixed, False
    )
    grad_query = grad_query.astype(jnp.bfloat16)
    grad_keyval = jnp.concatenate([grad_keys, grad_values], axis=1).astype(jnp.bfloat16)
    grad_normed = jnp.dot(grad_query, weight[:, :width].T, preferred_element_type=jnp.float32)
    grad_memory = jnp.dot(
        grad_keyval, weight[:, width : 3 * width].T, preferred_element_type=jnp.float32
    )
    grad_stream, gain_grad = rms_backward(stream, scale, gain, grad_normed)
    return (
        upstream + grad_stream,
        grad_memory.astype(jnp.bfloat16),
        gain_grad,
        (grad_out, grad_query, grad_keyval),
    )


def cross_weights(kept, grads, memory):
    grad_out, grad_query, grad_keyval = grads
    first = jnp.einsum("td,te->de", kept[0], grad_query, preferred_element_type=jnp.float32)
    middle = jnp.einsum("td,te->de", memory, grad_keyval, preferred_element_type=jnp.float32)
    last = jnp.einsum("td,te->de", kept[5], grad_out, preferred_element_type=jnp.float32)
    return jnp.concatenate([first, middle, last], axis=1)


def ffn_forward(stream, gain, weight_in, weight_out):
    normed, scale = rms_forward(stream, gain)
    normed = normed.astype(jnp.bfloat16)
    upward = jnp.dot(normed, weight_in, preferred_element_type=jnp.float32)
    hidden = jax.nn.gelu(upward, approximate=True).astype(jnp.bfloat16)
    result = stream + jnp.einsum(
        "tf,df->td", hidden, weight_out, preferred_element_type=jnp.float32
    )
    return (result, (normed, scale, upward, hidden))


def ffn_backward(stream, gain, weight_in, weight_out, kept, upstream):
    normed, scale, upward, hidden = kept
    grad_out = upstream.astype(jnp.bfloat16)
    grad_hidden = jnp.dot(grad_out, weight_out, preferred_element_type=jnp.float32)
    grad_up = (grad_hidden * gelu_slope(upward)).astype(jnp.bfloat16)
    grad_normed = jnp.einsum("tf,df->td", grad_up, weight_in, preferred_element_type=jnp.float32)
    grad_stream, gain_grad = rms_backward(stream, scale, gain, grad_normed)
    return (upstream + grad_stream, gain_grad, (grad_out, grad_up))


def ffn_weights(kept, grads):
    grad_out, grad_up = grads
    grad_in = jnp.einsum("td,tf->df", kept[0], grad_up, preferred_element_type=jnp.float32)
    grad_out_t = jnp.einsum("td,tf->df", grad_out, kept[3], preferred_element_type=jnp.float32)
    return (grad_in, grad_out_t)


def fetch_kept(store, tick_key, template):
    if tick_key in store:
        return store[tick_key]
    return jax.tree.map(jnp.zeros_like, template)


def join_tokens(pieces):
    return jax.tree.map(lambda *leaves: jnp.concatenate(leaves, axis=0), *pieces)


def per_device(section_ins, segments, buckets, section_mats, gains, tables):
    section = lax.axis_index("section")
    local_in = section_ins[0]
    mats = section_mats[0]
    rows_all, length = segments.shape
    width = local_in.shape[1]
    rows_micro = rows_all // MICRO
    tokens_micro = rows_micro * length
    attention_section = section % 2 == 0
    causal = section == 2
    table_index = section // 2
    gain_index = jnp.where(section == 0, 0, 3)
    self_gain = gains[gain_index]
    bias, onehot = distance_bias(tables[table_index], buckets[table_index], length)
    gain_rows = jnp.arange(gains.shape[0], dtype=jnp.int32)
    table_rows = jnp.arange(tables.shape[0], dtype=jnp.int32)
    gain_acc = jnp.zeros(gains.shape, jnp.float32)
    table_acc = jnp.zeros(tables.shape, jnp.float32)
    out_buffer = jnp.zeros((rows_all * length, width), jnp.float32)
    blank = jnp.zeros((tokens_micro, width), jnp.bfloat16)
    zeros_wide = jnp.zeros((tokens_micro, width), jnp.float32)
    never = jnp.asarray(False)
    forward_a, forward_b, backward_a, backward_b = (blank, blank, blank, blank)
    kept_self = {}
    kept_tail = {}
    record_self = {}
    record_tail = {}
    record_dec = {}

    def in_range(micro_index):
        micro_index = jnp.asarray(micro_index, jnp.int32)
        return (micro_index >= 0) & (micro_index < MICRO)

    def micro_slice(micro_index):
        start = jnp.clip(jnp.asarray(micro_index, jnp.int32), 0, MICRO - 1) * rows_micro
        segs = lax.dynamic_slice_in_dim(segments, start, rows_micro, 0)
        piece = lax.dynamic_slice_in_dim(local_in, start * length, tokens_micro, 0).astype(
            jnp.float32
        )
        return (segs, piece)

    def attention_head(stream, segs):
        return self_forward(stream, self_gain, mats[0], bias, segs, causal)

    def encoder_tail(received):
        stream = received.astype(jnp.float32)
        middle, ffn_kept = ffn_forward(stream, gains[1], mats[0], mats[1])
        encoded, final_scale = rms_forward(middle, gains[2])
        return (encoded, (ffn_kept, middle, final_scale, stream))

    def decoder_tail(received, memory_in, upstream, segs):
        stream = received.astype(jnp.float32)
        crossed, cross_kept = cross_forward(stream, memory_in, gains[4], mats[0], segs)
        final_in, ffn_kept = ffn_forward(crossed, gains[5], mats[1], mats[2])
        decoded, final_scale = rms_forward(final_in, gains[6])
        grad_final, gain_six = rms_backward(final_in, final_scale, gains[6], upstream)
        grad_cross, gain_five, ffn_grads = ffn_backward(
            crossed, gains[5], mats[1], mats[2], ffn_kept, grad_final
        )
        grad_stream, grad_memory, gain_four, cross_grads = cross_backward(
            stream, gains[4], mats[0], segs, cross_kept, grad_cross
        )
        return (
            decoded,
            grad_stream.astype(jnp.bfloat16),
            grad_memory,
            (gain_four, gain_five, gain_six),
            (cross_kept, ffn_kept, cross_grads, ffn_grads, memory_in),
        )

    def self_back(upstream, kept, stream, segs):
        return self_backward(stream, self_gain, mats[0], bias, segs, causal, kept, upstream)

    def encoder_back(extra, upstream, kept):
        ffn_kept, middle, final_scale, stream = kept
        grad_middle, gain_two = rms_backward(
            middle, final_scale, gains[2], upstream + extra.astype(jnp.float32)
        )
        grad_stream, gain_one, ffn_grads = ffn_backward(
            stream, gains[1], mats[0], mats[1], ffn_kept, grad_middle
        )
        return (grad_stream.astype(jnp.bfloat16), (gain_one, gain_two), ffn_grads)

    def branch_self(items):
        first = self_weights(items[0], items[1])
        empty = jnp.zeros_like(first)
        return jnp.stack([first, empty, empty])

    def branch_encoder(items):
        grad_in, grad_out_t = ffn_weights(items[2][0], items[3])
        return jnp.stack([grad_in, grad_out_t, jnp.zeros_like(grad_in)])

    def branch_decoder(items):
        cross_kept, ffn_kept, cross_grads, ffn_grads, memory_in = items[4]
        first = cross_weights(cross_kept, cross_grads, memory_in)
        grad_in, grad_out_t = ffn_weights(ffn_kept, ffn_grads)
        return jnp.stack([first, grad_in, grad_out_t])

    for tick in range(MICRO + 6):
        attn_out, encoded, decoded, self_stream = (zeros_wide, zeros_wide, zeros_wide, zeros_wide)
        back_stream, back_memory, back_first_in = (blank, blank, blank)
        ok_tail, ok_dec, ok_back_self = (never, never, never)
        if tick <= MICRO + 1:
            segs_self, piece_self = micro_slice(tick - section)
            ok_self = attention_section & in_range(tick - section)
            attn_out, attn_kept = only_on(ok_self, attention_head, piece_self, segs_self)
            kept_self[tick] = (attn_kept, piece_self, segs_self)
        if 1 <= tick <= MICRO:
            ok_tail = (section == 1) & in_range(tick - 1)
            encoded, tail_kept = only_on(ok_tail, encoder_tail, forward_a)
            kept_tail[tick] = tail_kept
        if 3 <= tick <= MICRO + 2:
            segs_dec, piece_dec = micro_slice(tick - 3)
            ok_dec = (section == 3) & in_range(tick - 3)
            decoded, back_stream, back_memory, gains_three, dec_kept = only_on(
                ok_dec, decoder_tail, forward_b, forward_a, piece_dec, segs_dec
            )
            record_dec[tick] = dec_kept
            gain_acc = (
                gain_acc.at[4]
                .add(gains_three[0])
                .at[5]
                .add(gains_three[1])
                .at[6]
                .add(gains_three[2])
            )
        if 4 <= tick <= MICRO + 5:
            early = fetch_kept(kept_self, tick - 6, kept_self[0])
            late = fetch_kept(kept_self, tick - 2, kept_self[0])
            chosen = jax.tree.map(
                lambda first, second: jnp.where(section == 0, first, second), early, late
            )
            ok_back_self = (section == 0) & in_range(tick - 6) | (section == 2) & in_range(tick - 4)
            upstream_self = jnp.where(section == 0, backward_a, backward_b).astype(jnp.float32)
            self_stream, self_gain_grad, diagonal, self_grads = only_on(
                ok_back_self, self_back, upstream_self, chosen[0], chosen[1], chosen[2]
            )
            record_self[tick] = (chosen[0], self_grads)
            gain_acc = (
                gain_acc + (gain_rows == gain_index).astype(jnp.float32)[:, None] * self_gain_grad
            )
            table_piece = jnp.dot(onehot.T, diagonal.T, precision=highest)
            table_acc = (
                table_acc
                + (table_rows == table_index).astype(jnp.float32)[:, None, None] * table_piece
            )
        if 5 <= tick <= MICRO + 4:
            tail_old = kept_tail[tick - 4]
            segs_unused, cot_piece = micro_slice(tick - 5)
            ok_back_tail = (section == 1) & in_range(tick - 5)
            back_first_in, gains_one, enc_grads = only_on(
                ok_back_tail, encoder_back, backward_a, cot_piece, tail_old
            )
            record_tail[tick] = (tail_old, enc_grads)
            gain_acc = gain_acc.at[1].add(gains_one[0]).at[2].add(gains_one[1])
        if tick <= MICRO + 1:
            send_a = jnp.where(
                section == 0,
                attn_out.astype(jnp.bfloat16),
                jnp.where(
                    section == 1,
                    encoded.astype(jnp.bfloat16),
                    jnp.where(section == 2, forward_a, blank),
                ),
            )
            send_b = jnp.where(section == 2, attn_out.astype(jnp.bfloat16), blank)
            forward_a, forward_b = passed_along((send_a, send_b), "section", 1)
        if 3 <= tick <= MICRO + 4:
            send_a = jnp.where(
                section == 3,
                back_memory,
                jnp.where(section == 2, backward_a, jnp.where(section == 1, back_first_in, blank)),
            )
            send_b = jnp.where(section == 3, back_stream, blank)
            backward_a, backward_b = passed_along((send_a, send_b), "section", -1)
        out_piece = self_stream + encoded + decoded
        out_micro = jnp.where(
            section == 0,
            tick - 6,
            jnp.where(section == 1, tick - 1, jnp.where(section == 2, tick - 4, tick - 3)),
        )
        ok_out = ok_back_self | ok_tail | ok_dec
        start = jnp.clip(out_micro, 0, MICRO - 1) * tokens_micro
        previous = lax.dynamic_slice_in_dim(out_buffer, start, tokens_micro, 0)
        out_buffer = lax.dynamic_update_slice_in_dim(
            out_buffer, jnp.where(ok_out, out_piece, previous), start, 0
        )

    def micro_items(micro_index):
        self_pair = jax.tree.map(
            lambda first, second: jnp.where(section == 0, first, second),
            record_self[6 + micro_index],
            record_self[4 + micro_index],
        )
        tail_pair = record_tail[5 + micro_index]
        return (self_pair[0], self_pair[1], tail_pair[0], tail_pair[1], record_dec[3 + micro_index])

    joined = join_tokens([micro_items(micro_index) for micro_index in range(MICRO)])
    weight_acc = jax.tree.map(
        lambda part: part.astype(jnp.float32),
        lax.psum_scatter(
            for_sending(
                lax.switch(
                    section, [branch_self, branch_encoder, branch_self, branch_decoder], joined
                )
            ),
            "dp",
            scatter_dimension=1,
            tiled=True,
        ),
    )
    gain_total, table_total = lax.psum((gain_acc, table_acc), ("section", "dp"))
    return (out_buffer[None], weight_acc[None], gain_total, table_total)


def solution(mesh):
    placed = (
        P("section", "dp", None),
        P("dp", None),
        P(),
        P("section", None, None, None),
        P(),
        P(),
    )
    return jax.shard_map(
        per_device,
        mesh=mesh,
        in_specs=placed,
        out_specs=(P("section", "dp", None), P("section", None, "dp", None), P(), P()),
        check_vma=False,
    )
```

profile of v0, /device:TPU:2, one launch (start us, length us, event | category | flops | bytes accessed | tf_op | source)
XLA Modules:
  0.0 1379.7 jit_solution(17584380088325128547)
XLA Ops:
  9.1 11.6 tile.4
  20.7 10.9 pad.107
  31.6 39.8 %copy.272 = f32[2,8,512,1024]{3,1,2,0:T(8,128)} copy(f32[2,8,512,1024]{3,2,1,0:T(8,128)S(1)} %bitcast.469) | data formatting | bytes 67108864
  71.4 22.6 %slice.554 = f32[12,523776]{1,0:T(8,128)} slice(f32[12,524288]{1,0:T(8,128)} %bitcast.470), slice={[0:12], [0:523776]} | slice | bytes 50282496 | tf_op jit(solution)/shard_map/slice | solution.py:59
  94.0 51.7 %reshape.1712 = f32[12,512,1023]{2,1,0:T(8,128)} reshape(f32[12,523776]{1,0:T(8,128)} %slice.554) | data formatting | bytes 50282496 | tf_op jit(solution)/shard_map/reshape | solution.py:60
  145.8 13.5 slice.555
  170.4 4.4 conditional.17
  174.8 7.2 collective-permute-done
  182.1 10.5 conditional.16
  197.4 47.6 %conditional.19 = (bf16[512,768]{1,0:T(8,128)(2,1)}, f32[512,1]{0,1:T(1,128)S(1)}, bf16[512,2304]{1,0:T(8,128)(2,1)}, f32[1,12,512]{2,1,0:T(8,128)S(1)}, bf16[51...) conditional(s32[]{:T(128)} %convert_element_type.487, () %tuple.235, (f32[512,768]{1,0:T(8,128)S(1)}, ...), branch_computations={%region_18.19_spmd, %region_19.23_spmd} | conditional | flops 3251759616 | bytes 209161520 | solution.py:53
  209.9 12.6 copy.179
  222.7 6.1 fusion.272
  233.8 7.0 fusion.51
  245.0 10.5 collective-permute-done.1
  255.5 6.8 conditional.18
  271.2 44.9 %collective-permute-start.11 = (bf16[512,768]{1,0:T(8,128)(2,1)}, bf16[512,768]{1,0:T(8,128)(2,1)}, u32[]{:S(2)}, u32[]{:S(2)}) collective-permute-start(bf16[512,768]{1,0:T(8,128)(2,1)} %select_n.570), channel_id=1, source_target_pairs={{8,0},{16,8},{24,16},{9,1},{17,9},{25,17},{10,2},{18,10},{26,18},{... | collective-permute-start | bytes 2359304 | tf_op jit(solution)/shard_map/ppermute | solution.py:19
  320.8 49.0 %conditional.22 = (bf16[512,768]{1,0:T(8,128)(2,1)}, f32[512,1]{0,1:T(1,128)S(1)}, bf16[512,2304]{1,0:T(8,128)(2,1)}, f32[1,12,512]{2,1,0:T(8,128)S(1)}, bf16[51...) conditional(s32[]{:T(128)} %convert_element_type.495, () %tuple.241, (f32[512,768]{1,0:T(8,128)S(1)}, ...), branch_computations={%region_43.44_spmd, %region_44.48_spmd} | conditional | flops 3251759616 | bytes 209161520 | solution.py:53
  334.4 12.7 copy.183
  347.4 6.3 fusion.274
  358.5 7.0 fusion.133
  379.7 25.4 %conditional.20 = (f32[512,768]{1,0:T(8,128)}, bf16[512,768]{1,0:T(8,128)(2,1)}, bf16[512,768]{1,0:T(8,128)(2,1)}, bf16[512,768]{1,0:T(8,128)(2,1)}, bf16[512,76...) conditional(s32[]{:T(128)} %convert_element_type.486, ...), branch_computations={%region_23.24_spmd, %region_24.37_spmd} | conditional | flops 17056784384 | bytes 488353568 | solution.py:53
  416.7 6.0 pad_maximum_fusion.14
  422.7 24.8 %conditional.23 = (f32[512,768]{1,0:T(8,128)}, bf16[512,768]{1,0:T(8,128)(2,1)}, bf16[512,768]{1,0:T(8,128)(2,1)}, bf16[512,768]{1,0:T(8,128)(2,1)}, bf16[512,76...) conditional(s32[]{:T(128)} %convert_element_type.486, ...), branch_computations={%region_48.49_spmd, %region_49.62_spmd} | conditional | flops 17056784384 | bytes 488328992 | solution.py:53
  461.9 205.1 %conditional.21 = (f32[512,768]{1,0:T(8,128)}, f32[768]{0:T(1024)}, f32[12,1023]{1,0:T(8,128)}, bf16[512,768]{1,0:T(8,128)(2,1)}, bf16[512,2304]{1,0:T(8,128)(2,1)}) conditional(s32[]{:T(128)} %convert_element_type.493, () %tuple.238, (pred[]{:T(512)}, f32[512,1]{0,1:T(1,128)S(1)}, f32[512,1]{0,1:T(1,128)}, f32[1,768]{1,0:T(1,128)S(1)}, ...), branch_computations={%region_37.38_spmd, %region_38.43_spmd} | conditional | flops 4493518336 | bytes 522070048 | solution.py:53
  474.0 4.3 copy.181
  485.2 6.3 fusion.288
  491.6 12.6 copy.182
  505.2 14.9 %multiply_reduce_fusion.14 = (f32[12,512]{1,0:T(8,128)S(1)}, f32[12,512,512]{1,2,0:T(8,128)}) fusion(f32[12,512,512]{1,2,0:T(8,128)} %fusion.288, f32[12,512]{1,0:T(8,128)S(1)} %select_bitcast_fusion, f32[12,512,512]{1,2,0:T(8,128)} %copy.182, bf16[512,12,64]{0,2,1:T(8,128)(2,1)} %bitcast.516, bf16[512,12,64]{0,2,1:T(8,128)(2,1)S(1)} %bitcast.496, ...), kind=kOutput, calls=%fused_computation.217 | convolution fusion | flops 418375680 | bytes 39632896 | tf_op jit(solution)/shard_map/cond/branch_1_fun/while/body/eval_jaxpr/ihd,jhd->hij/dot_general | solution.py:133
  521.9 6.8 multiply_convert_fusion.7
  539.6 15.9 %copy.248 = bf16[512,2304]{1,0:T(8,128)(2,1)} copy(bf16[512,2304]{0,1:T(8,128)(2,1)S(1)} %pad_maximum_fusion.3) | data formatting | bytes 4718592 | tf_op jit(solution)/shard_map/cond | solution.py:53
  556.2 6.9 multiply_reduce_fusion.15
  564.8 8.7 copy.263
  573.4 10.6 concatenate.101.clone
  584.0 34.7 %reshape.1666 = bf16[12,523776]{1,0:T(8,128)(2,1)} reshape(bf16[12,512,1023]{2,1,0:T(8,128)(2,1)} %concatenate.101.clone) | data formatting | bytes 25141248 | tf_op jit(solution)/shard_map/cond/branch_1_fun/reshape | solution.py:66
  618.7 8.8 concatenate.102
  627.6 25.7 %copy.268 = bf16[2,8,512,1024]{3,2,1,0:T(8,128)(2,1)S(1)} copy(bf16[2,8,512,1024]{3,1,2,0:T(8,128)(2,1)S(1)} %bitcast.484) | data formatting | bytes 33554432 | tf_op jit(solution)/shard_map/cond
  653.3 5.2 slice.564
  658.5 8.3 convert_reduce_fusion
  674.5 4.0 pad_maximum_fusion.18
  679.1 4.0 select_select_fusion.5
  689.0 12.0 pad_maximum_fusion.15
  708.3 15.3 %collective-permute-start.12 = (bf16[512,768]{1,0:T(8,128)(2,1)}, bf16[512,768]{1,0:T(8,128)(2,1)}, u32[]{:S(2)}, u32[]{:S(2)}) collective-permute-start(bf16[512,768]{1,0:T(8,128)(2,1)} %select_select_fusion.4), channel_id=1, source_target_pairs={{8,0},{16,8},{24,16},{9,1},{17,9},{25,17},{10,2},{18,10},{26,18},{... | collective-permute-start | bytes 2359304 | tf_op jit(solution)/shard_map/ppermute | solution.py:19
  726.3 191.8 %conditional.24 = (f32[512,768]{1,0:T(8,128)}, f32[768]{0:T(1024)}, f32[12,1023]{1,0:T(8,128)}, bf16[512,768]{1,0:T(8,128)(2,1)}, bf16[512,2304]{1,0:T(8,128)(2,1)}) conditional(s32[]{:T(128)} %convert_element_type.493, () %tuple.244, (pred[]{:T(512)}, f32[512,1]{0,1:T(1,128)S(1)}, f32[512,1]{0,1:T(1,128)}, f32[1,768]{1,0:T(1,128)S(1)}, ...), branch_computations={%region_62.63_spmd, %region_63.68_spmd} | conditional | flops 4493518336 | bytes 522070048 | solution.py:53
  738.5 4.3 copy.185
  749.7 6.3 fusion.289
  756.0 12.6 copy.186
  769.6 14.8 %multiply_reduce_fusion.25 = (f32[12,512]{1,0:T(8,128)S(1)}, f32[12,512,512]{1,2,0:T(8,128)}) fusion(f32[12,512,512]{1,2,0:T(8,128)} %fusion.289, f32[12,512]{1,0:T(8,128)S(1)} %select_bitcast_fusion.1, f32[12,512,512]{1,2,0:T(8,128)} %copy.186, bf16[512,12,64]{0,2,1:T(8,128)(2,1)} %bitcast.518, bf16[512,12,64]{0,2,1:T(8,128)(2,1)S(1)} %bitcast.498, ...), kind=kOutput, calls=%fused_computation.364 | convolution fusion | flops 418375680 | bytes 39632896 | tf_op jit(solution)/shard_map/cond/branch_1_fun/while/body/eval_jaxpr/ihd,jhd->hij/dot_general | solution.py:133
  786.3 6.8 multiply_convert_fusion.11
  807.5 6.9 multiply_reduce_fusion.26
  816.1 8.7 copy.264
  824.7 10.6 concatenate.105.clone
  835.3 34.5 %reshape.1687 = bf16[12,523776]{1,0:T(8,128)(2,1)} reshape(bf16[12,512,1023]{2,1,0:T(8,128)(2,1)} %concatenate.105.clone) | data formatting | bytes 25141248 | tf_op jit(solution)/shard_map/cond/branch_1_fun/reshape | solution.py:66
  869.8 8.8 concatenate.106
  878.7 25.7 %copy.269 = bf16[2,8,512,1024]{3,2,1,0:T(8,128)(2,1)S(1)} copy(bf16[2,8,512,1024]{3,1,2,0:T(8,128)(2,1)S(1)} %bitcast.485) | data formatting | bytes 33554432 | tf_op jit(solution)/shard_map/cond
  904.4 5.2 slice.565
  909.6 8.3 convert_reduce_fusion.1
  920.9 5.3 pad_maximum_fusion.13
  928.9 13.8 %conditional.26 = (f32[512,768]{1,0:T(8,128)}, f32[768]{0:T(1024)}, f32[12,1023]{1,0:T(8,128)}, bf16[512,768]{1,0:T(8,128)(2,1)}, bf16[512,2304]{1,0:T(8,128)(2,1)}) conditional(s32[]{:T(128)} %convert_element_type.501, () %tuple.246, (pred[]{:T(512)}, f32[512,1]{0,1:T(1,128)}, f32[512,1]{0,1:T(1,128)S(1)}, f32[1,768]{1,0:T(1,128)S(1)}, ...), branch_computations={%region_74.75_spmd, %region_75.80_spmd} | conditional | flops 4493518336 | bytes 522070048 | solution.py:53
  942.7 20.8 %conditional.28 = (f32[512,768]{1,0:T(8,128)}, f32[768]{0:T(1024)S(1)}, f32[12,1023]{1,0:T(8,128)}, bf16[512,768]{1,0:T(8,128)(2,1)}, bf16[512,2304]{1,0:T(8,128)(2,1)}) conditional(s32[]{:T(128)} %convert_element_type.501, () %tuple.250, (pred[]{:T(512)}, f32[512,1]{0,1:T(1,128)}, f32[512,1]{0,1:T(1,128)S(1)}, f32[1,768]{1,0:T(1,128)S(1)}, ...), branch_computations={%region_86.87_spmd, %region_87.92_spmd} | conditional | flops 4493518336 | bytes 529950880 | solution.py:53
  972.8 12.0 conditional.29
  973.0 4.2 fusion.283
  979.3 5.2 stack.28
  1001.6 199.2 %all-reduce.12 = (f32[7,768]{1,0:T(8,128)}, f32[2,32,12]{1,0,2:T(2,128)}) all-reduce(f32[7,768]{1,0:T(8,128)S(1)} %multiply_add_fusion.4, f32[2,32,12]{1,0,2:T(2,128)S(1)} %broadcast_multiply_fusion.14), channel_id=1, replica_groups=mesh['section'=4,'dp'=8] {'section','dp'}, use_global_device_ids=true, to_apply=%region_97.98 | all-reduce | flops 6144 | bytes 49152 | tf_op jit(solution)/shard_map/psum | solution.py:545
  1202.2 166.5 %reduce-scatter.2.cloned.1.call-done = bf16[3,96,3072]{2,1,0:T(8,128)(2,1)} async-done(((bf16[3,768,3072]{2,1,0:T(8,128)(2,1)}), bf16[3,96,3072]{2,1,0:T(8,128)(2,1)}) %reduce-scatter.2.cloned.1.call-update) | async-done | bytes 1769488 | tf_op jit(solution)/shard_map/reduce_scatter | solution.py:534
  (531 shorter events, 312.7 us)
Async XLA Ops:
  7.2 1361.6 %reduce-scatter.2.cloned.1.call-start = ((), (), s32[]{:S(2)}) async-start(), calls=%async_computation.1 | async-start | bytes 15925248 | tf_op jit(solution)/shard_map/reduce_scatter | solution.py:534
  8.6 12.1 copy-start.213
  145.7 13.5 copy-start.165
  145.8 14.1 %copy-start.156 = (f32[7,768]{1,0:T(8,128)S(1)}, f32[7,768]{1,0:T(8,128)}, u32[]{:S(2)}) copy-start(f32[7,768]{1,0:T(8,128)} %param.62) | copy-start | bytes 64516
  145.8 14.1 %copy-start.49 = (bf16[1,1024,768]{2,1,0:T(8,128)(2,1)S(1)}, bf16[1,1024,768]{2,1,0:T(8,128)(2,1)}, u32[]{:S(2)}) copy-start(bf16[1,1024,768]{2,1,0:T(8,128)(2,1)} %param.58) | copy-start | bytes 4718596
  159.9 10.5 copy-start.171
  159.9 37.5 %copy-start.177 = (s32[1,512]{1,0:T(1,128)}, s32[1,512]{1,0:T(1,128)S(1)}, u32[]{:S(2)}) copy-start(s32[1,512]{1,0:T(1,128)S(1)} %get-tuple-element.1755) | copy-start | bytes 6148
  159.9 160.9 %copy-start.144 = (f32[1,768]{1,0:T(1,128)}, f32[1,768]{1,0:T(1,128)S(1)}, u32[]{:S(2)}) copy-start(f32[1,768]{1,0:T(1,128)S(1)} %constant_dynamic-slice_fusion.6) | copy-start | bytes 9220
  168.4 13.6 collective-permute-start
  195.4 60.1 %collective-permute-start.1 = (bf16[512,768]{1,0:T(8,128)(2,1)}, bf16[512,768]{1,0:T(8,128)(2,1)}, u32[]{:S(2)}, u32[]{:S(2)}) collective-permute-start(bf16[512,768]{1,0:T(8,128)(2,1)} %select_select_fusion.9), channel_id=1, source_target_pairs={{0,8},{8,16},{16,24},{1,9},{9,17},{17,25},{2,10},{10,18},{18,26},{... | collective-permute-start | bytes 2359304 | tf_op jit(solution)/shard_map/ppermute | solution.py:19
  245.0 10.5 copy-start.152
  245.0 10.5 copy-start.188
  262.3 58.5 %copy-start.31 = (f32[512,768]{1,0:T(8,128)}, f32[512,768]{1,0:T(8,128)S(1)}, u32[]{:S(2)}) copy-start(f32[512,768]{1,0:T(8,128)S(1)} %get-tuple-element.1143) | copy-start | bytes 4718596
  262.3 55.8 %copy-start.112 = (bf16[512,768]{1,0:T(8,128)(2,1)S(1)}, bf16[512,768]{1,0:T(8,128)(2,1)}, u32[]{:S(2)}) copy-start(bf16[512,768]{1,0:T(8,128)(2,1)} %copy-done.111) | copy-start | bytes 2359300
  268.2 52.6 %copy-start.43 = (f32[512,768]{1,0:T(8,128)S(1)}, f32[512,768]{1,0:T(8,128)}, u32[]{:S(2)}) copy-start(f32[512,768]{1,0:T(8,128)} %get-tuple-element.1743) | copy-start | bytes 4718596
  268.2 52.6 %copy-start.175 = (s32[1,512]{1,0:T(1,128)S(1)}, s32[1,512]{1,0:T(1,128)}, u32[]{:S(2)}) copy-start(s32[1,512]{1,0:T(1,128)} %get-tuple-element.1754) | copy-start | bytes 6148
  268.2 104.9 %collective-permute-start.3 = (bf16[512,768]{1,0:T(8,128)(2,1)}, bf16[512,768]{1,0:T(8,128)(2,1)}, u32[]{:S(2)}, u32[]{:S(2)}) collective-permute-start(bf16[512,768]{1,0:T(8,128)(2,1)} %get-tuple-element.1752), channel_id=1, source_target_pairs={{0,8},{8,16},{16,24},{1,9},{9,17},{17,25},{2,10},{10,18},{18,26},{... | collective-permute-start | bytes 2359304 | tf_op jit(solution)/shard_map/ppermute | solution.py:19
  271.2 655.0 %collective-permute-start.11 = (bf16[512,768]{1,0:T(8,128)(2,1)}, bf16[512,768]{1,0:T(8,128)(2,1)}, u32[]{:S(2)}, u32[]{:S(2)}) collective-permute-start(bf16[512,768]{1,0:T(8,128)(2,1)} %select_n.570), channel_id=1, source_target_pairs={{8,0},{16,8},{24,16},{9,1},{17,9},{25,17},{10,2},{18,10},{26,18},{... | collective-permute-start | bytes 2359304 | tf_op jit(solution)/shard_map/ppermute | solution.py:19
  316.2 63.5 %collective-permute-start.2 = (bf16[512,768]{1,0:T(8,128)(2,1)}, bf16[512,768]{1,0:T(8,128)(2,1)}, u32[]{:S(2)}, u32[]{:S(2)}) collective-permute-start(bf16[512,768]{1,0:T(8,128)(2,1)} %get-tuple-element.1753), channel_id=1, source_target_pairs={{0,8},{8,16},{16,24},{1,9},{9,17},{17,25},{2,10},{10,18},{18,26},{... | collective-permute-start | bytes 2359304 | tf_op jit(solution)/shard_map/ppermute | solution.py:19
  329.1 18.0 %copy-start.29 = (bf16[512,2304]{1,0:T(8,128)(2,1)}, bf16[512,2304]{1,0:T(8,128)(2,1)S(1)}, u32[]{:S(2)}) copy-start(bf16[512,2304]{1,0:T(8,128)(2,1)S(1)} %convolution_convert_fusion.11) | copy-start | bytes 7077892 | tf_op jit(solution)/shard_map/cond
  375.8 46.9 %collective-permute-start.6 = (bf16[512,768]{1,0:T(8,128)(2,1)}, bf16[512,768]{1,0:T(8,128)(2,1)}, u32[]{:S(2)}, u32[]{:S(2)}) collective-permute-start(bf16[512,768]{1,0:T(8,128)(2,1)} %get-tuple-element.1751), channel_id=1, source_target_pairs={{0,8},{8,16},{16,24},{1,9},{9,17},{17,25},{2,10},{10,18},{18,26},{... | collective-permute-start | bytes 2359304 | tf_op jit(solution)/shard_map/ppermute | solution.py:19
  377.7 44.9 %collective-permute-start.7 = (bf16[512,768]{1,0:T(8,128)(2,1)}, bf16[512,768]{1,0:T(8,128)(2,1)}, u32[]{:S(2)}, u32[]{:S(2)}) collective-permute-start(bf16[512,768]{1,0:T(8,128)(2,1)} %get-tuple-element.1750), channel_id=1, source_target_pairs={{0,8},{8,16},{16,24},{1,9},{9,17},{17,25},{2,10},{10,18},{18,26},{... | collective-permute-start | bytes 2359304 | tf_op jit(solution)/shard_map/ppermute | solution.py:19
  405.1 10.3 copy-start.146
  405.1 10.3 copy-start.194
  405.1 10.3 copy-start.196
  405.1 10.3 copy-start.105
  405.2 10.3 copy-start.107
  406.1 41.5 %collective-permute-start.4 = (bf16[512,768]{1,0:T(8,128)(2,1)}, bf16[512,768]{1,0:T(8,128)(2,1)}, u32[]{:S(2)}, u32[]{:S(2)}) collective-permute-start(bf16[512,768]{1,0:T(8,128)(2,1)} %broadcast_select_fusion.8), channel_id=1, source_target_pairs={{8,0},{16,8},{24,16},{9,1},{17,9},{25,17},{10,2},{18,10},{26,18},{... | collective-permute-start | bytes 2359304 | tf_op jit(solution)/shard_map/ppermute | solution.py:19
  410.9 36.7 %collective-permute-start.5 = (bf16[512,768]{1,0:T(8,128)(2,1)}, bf16[512,768]{1,0:T(8,128)(2,1)}, u32[]{:S(2)}, u32[]{:S(2)}) collective-permute-start(bf16[512,768]{1,0:T(8,128)(2,1)} %broadcast_select_fusion.7), channel_id=1, source_target_pairs={{8,0},{16,8},{24,16},{9,1},{17,9},{25,17},{10,2},{18,10},{26,18},{... | collective-permute-start | bytes 2359304 | tf_op jit(solution)/shard_map/ppermute | solution.py:19
  450.1 228.4 %collective-permute-start.8 = (bf16[512,768]{1,0:T(8,128)(2,1)}, bf16[512,768]{1,0:T(8,128)(2,1)}, u32[]{:S(2)}, u32[]{:S(2)}) collective-permute-start(bf16[512,768]{1,0:T(8,128)(2,1)} %get-tuple-element.1748), channel_id=1, source_target_pairs={{8,0},{16,8},{24,16},{9,1},{17,9},{25,17},{10,2},{18,10},{26,18},{... | collective-permute-start | bytes 2359304 | tf_op jit(solution)/shard_map/ppermute | solution.py:19
  453.0 226.1 %collective-permute-start.9 = (bf16[512,768]{1,0:T(8,128)(2,1)}, bf16[512,768]{1,0:T(8,128)(2,1)}, u32[]{:S(2)}, u32[]{:S(2)}) collective-permute-start(bf16[512,768]{1,0:T(8,128)(2,1)} %broadcast_select_fusion.6), channel_id=1, source_target_pairs={{8,0},{16,8},{24,16},{9,1},{17,9},{25,17},{10,2},{18,10},{26,18},{... | collective-permute-start | bytes 2359304 | tf_op jit(solution)/shard_map/ppermute | solution.py:19
  491.6 12.6 copy-start.157
  491.6 12.6 copy-start.161
  491.6 12.6 copy-start.178
  491.6 13.6 copy-start.133
  491.6 13.6 copy-start.153
  505.2 14.9 %slice-start.18 = ((s8[12582912]{0:T(1024)(128)(4,1)}), s8[4194304]{0:T(1024)(128)(4,1)S(1)}, s32[]{:S(2)}) async-start(s8[12582912]{0:T(1024)(128)(4,1)} %bitcast.471), calls=%async_computation.20 | async-start | bytes 8388608 | tf_op jit(solution)/shard_map/cond
  505.2 14.9 %slice-start.19 = ((s8[12582912]{0:T(1024)(128)(4,1)}), s8[4194304]{0:T(1024)(128)(4,1)S(1)}, s32[]{:S(2)}) async-start(s8[12582912]{0:T(1024)(128)(4,1)} %bitcast.471), calls=%async_computation.21 | async-start | bytes 8388608 | tf_op jit(solution)/shard_map/cond
  505.2 16.7 %slice-start.20 = ((s8[12582912]{0:T(1024)(128)(4,1)}), s8[4194304]{0:T(1024)(128)(4,1)S(1)}, s32[]{:S(2)}) async-start(s8[12582912]{0:T(1024)(128)(4,1)} %bitcast.471), calls=%async_computation.22 | async-start | bytes 8388608 | tf_op jit(solution)/shard_map/cond
  679.1 9.8 copy-start.52
  683.1 17.9 %collective-permute-start.10 = (bf16[512,768]{1,0:T(8,128)(2,1)S(1)}, bf16[512,768]{1,0:T(8,128)(2,1)}, u32[]{:S(2)}, u32[]{:S(2)}) collective-permute-start(bf16[512,768]{1,0:T(8,128)(2,1)S(1)} %get-tuple-element.1746), channel_id=1, source_target_pairs={{8,0},{16,8},{24,16},{9,1},{17,9},{25,17},{10,2},{18,10},{26,18},{... | collective-permute-start | bytes 2359304 | tf_op jit(solution)/shard_map/ppermute | solution.py:19
  685.1 16.0 %slice-start.6 = ((s8[14155776]{0:T(1024)(128)(4,1)}), s8[4194304]{0:T(1024)(128)(4,1)S(1)}, s32[]{:S(2)}) async-start(s8[14155776]{0:T(1024)(128)(4,1)} %bitcast.462), calls=%async_computation.8 | async-start | bytes 8388608
  685.1 15.9 %slice-start.34 = ((s8[6291456]{0:T(1024)(128)(4,1)}), s8[4194304]{0:T(1024)(128)(4,1)S(1)}, s32[]{:S(2)}) async-start(s8[6291456]{0:T(1024)(128)(4,1)} %bitcast.536), calls=%async_computation.36 | async-start | bytes 8388608
  689.0 12.1 slice-start.7
  689.0 12.1 slice-start.8
  689.0 12.1 slice-start.9
  689.0 13.1 copy-start.19
  689.0 13.8 slice-start.35
  689.0 13.8 copy-start.170
  705.4 20.8 %copy-start.56 = (bf16[512,3072]{1,0:T(8,128)(2,1)}, bf16[512,3072]{1,0:T(8,128)(2,1)S(1)}, u32[]{:S(2)}) copy-start(bf16[512,3072]{1,0:T(8,128)(2,1)S(1)} %get-tuple-element.1199) | copy-start | bytes 9437188
  705.4 20.8 %copy-start.208 = (f32[1,768]{1,0:T(1,128)}, f32[1,768]{1,0:T(1,128)S(1)}, u32[]{:S(2)}) copy-start(f32[1,768]{1,0:T(1,128)S(1)} %get-tuple-element.1235) | copy-start | bytes 9220
  705.5 20.8 %copy-start.210 = (f32[1,768]{1,0:T(1,128)}, f32[1,768]{1,0:T(1,128)S(1)}, u32[]{:S(2)}) copy-start(f32[1,768]{1,0:T(1,128)S(1)} %get-tuple-element.1236) | copy-start | bytes 9220
  705.5 20.8 %copy-start.15 = (bf16[512,2304]{0,1:T(8,128)(2,1)S(1)}, bf16[512,2304]{0,1:T(8,128)(2,1)}, u32[]{:S(2)}) copy-start(bf16[512,2304]{0,1:T(8,128)(2,1)} %copy-done.14) | copy-start | bytes 7077892
  705.5 20.8 %copy-start.34 = (f32[512,768]{1,0:T(8,128)S(1)}, f32[512,768]{1,0:T(8,128)}, u32[]{:S(2)}) copy-start(f32[512,768]{1,0:T(8,128)} %get-tuple-element.1747) | copy-start | bytes 4718596
  708.3 217.9 %collective-permute-start.12 = (bf16[512,768]{1,0:T(8,128)(2,1)}, bf16[512,768]{1,0:T(8,128)(2,1)}, u32[]{:S(2)}, u32[]{:S(2)}) collective-permute-start(bf16[512,768]{1,0:T(8,128)(2,1)} %select_select_fusion.4), channel_id=1, source_target_pairs={{8,0},{16,8},{24,16},{9,1},{17,9},{25,17},{10,2},{18,10},{26,18},{... | collective-permute-start | bytes 2359304 | tf_op jit(solution)/shard_map/ppermute | solution.py:19
  756.0 12.6 copy-start.158
  756.0 12.6 copy-start.162
  756.0 12.6 copy-start.176
  756.0 13.6 copy-start.134
  756.0 13.6 copy-start.155
  769.6 14.9 %slice-start.21 = ((s8[12582912]{0:T(1024)(128)(4,1)}), s8[4194304]{0:T(1024)(128)(4,1)S(1)}, s32[]{:S(2)}) async-start(s8[12582912]{0:T(1024)(128)(4,1)} %bitcast.473), calls=%async_computation.23 | async-start | bytes 8388608 | tf_op jit(solution)/shard_map/cond
  769.6 14.9 %slice-start.22 = ((s8[12582912]{0:T(1024)(128)(4,1)}), s8[4194304]{0:T(1024)(128)(4,1)S(1)}, s32[]{:S(2)}) async-start(s8[12582912]{0:T(1024)(128)(4,1)} %bitcast.473), calls=%async_computation.24 | async-start | bytes 8388608 | tf_op jit(solution)/shard_map/cond
  769.6 16.7 %slice-start.23 = ((s8[12582912]{0:T(1024)(128)(4,1)}), s8[4194304]{0:T(1024)(128)(4,1)S(1)}, s32[]{:S(2)}) async-start(s8[12582912]{0:T(1024)(128)(4,1)} %bitcast.473), calls=%async_computation.25 | async-start | bytes 8388608 | tf_op jit(solution)/shard_map/cond
  1200.8 171.6 %copy-start.1 = (f32[2,32,12]{1,0,2:T(2,128)S(1)}, f32[2,32,12]{1,0,2:T(2,128)}, u32[]{:S(2)}) copy-start(f32[2,32,12]{1,0,2:T(2,128)} %param.63) | copy-start | bytes 9220
  (85 other events, 354.6 us)
Sparse Core Ops, SparseCore 0:
  984.9 383.7 reduce-scatter.1
where the time goes:
time: 1390 us; the launch traced here: 1380 us
  local copies, waits for them, and re-layouts  569 us (41%)
  blocking collectives  199 us (14%)
  waiting for transfers between devices  184 us (13%)
  other arithmetic  155 us (11%)
  matrix products  123 us (9%)
  starting transfers between devices  84.6 us (6%)
  loops' own time  48.5 us (3%)
  between operations  16 us (1%)
    psum x1, blocking collectives, per_device(): gain_total, table_total = lax.psum((gain_acc, table_acc), ('section', 'dp'))  199 us
    reduce_scatter x1, waiting for transfers between devices, per_device(): lax.psum_scatter(for_sending(lax.switch(section, [branch_self, branch_enc...  167 us
    another operation x91, local copies, waits for them, and re-layouts  133 us
    cond x112, local copies, waits for them, and re-layouts  96.3 us
    ppermute x13, starting transfers between devices, passed_along(): lax.ppermute(value, axis, [(source, source + steps) for source in range(l...  84.6 us
    reshape x2, local copies, waits for them, and re-layouts, sum_diagonals(): shifted = shifted.reshape(heads, length * (2 * length - 1))  69.2 us
    unnamed x165, local copies, waits for them, and re-layouts  61.9 us
    reshape x1, local copies, waits for them, and re-layouts, spread_diagonals(): return tiled.reshape(heads, length, 2 * length - 1)[:, :, length - 1:]  51.7 us
  transfers between devices with their start and end apart: 14, of which 3 were waited for; matrix products, arithmetic and copies ran while one was open for 43% of the time, Pallas kernels for 0%

commit v1 on v0

v1 whole, which is shorter than its diff:
```python
from functools import partial

import jax
import jax.numpy as jnp
from jax import lax
from jax.experimental import pallas as pl
from jax.experimental.pallas import tpu as pltpu
from jax.sharding import PartitionSpec as P

H = 12
HD = 64
PAIRS = H // 2
EPS = 1e-06
GELU = 0.7978845608028654
CUBIC = 0.044715
MASKED = -1e38
F32 = jnp.float32
BF16 = jnp.bfloat16
ROW_STEP = 128
VMEM_LIMIT = 60 * 1024 * 1024


def mm(a, b):
    return jnp.dot(a, b, preferred_element_type=F32)


def mm_nt(a, b):
    return lax.dot_general(a, b, (((1,), (1,)), ((), ())), preferred_element_type=F32)


def inverse_rms(x):
    return lax.rsqrt(jnp.mean(x * x, axis=-1, keepdims=True) + EPS)


def row_chunks(length):
    return [pl.ds(start, ROW_STEP) for start in range(0, length, ROW_STEP)]


def rms_back(x, gain, dy):
    r = inverse_rms(x)
    inner = jnp.mean(dy * gain * x, axis=-1, keepdims=True)
    dx = r * gain * dy - x * (r * r * r) * inner
    return dx, jnp.sum(dy * x * r, axis=0, keepdims=True)


def copy_all(sems, first, *pairs):
    started = []
    for offset, (source, target) in enumerate(pairs):
        one = pltpu.make_async_copy(source, target, sems.at[first + offset])
        one.start()
        started.append(one)
    return started


def wait_all(started):
    for one in started:
        one.wait()


def head_lanes(second):
    lane = lax.broadcasted_iota(jnp.int32, (1, 2 * HD), 1)
    return (lane >= HD) if second else (lane < HD)


def fill_mask(mask_v, seg_row, transposed, slack):
    length = seg_row.shape[1]
    down = jnp.broadcast_to(seg_row, (128, length)).T
    for c in range(length // 128):
        along = seg_row[:, c * 128 : (c + 1) * 128]
        r = lax.broadcasted_iota(jnp.int32, (length, 128), 0)
        q = lax.broadcasted_iota(jnp.int32, (length, 128), 1) + c * 128
        key, query = (r, q) if transposed else (q, r)
        ok = (down == along) & (key <= query + slack)
        mask_v[:, c * 128 : (c + 1) * 128] = jnp.where(ok, 0.0, MASKED)


def fill_toeplitz(toe_v, vec_v, table, bucket_row):
    count = bucket_row.shape[1]
    ids = lax.broadcasted_iota(jnp.int32, (table.shape[1], count), 0)
    onehot = (ids == bucket_row).astype(F32)
    vec = jnp.dot(table, onehot, precision=lax.Precision.HIGHEST, preferred_element_type=F32)
    vec_v[:, :count] = vec

    @pl.loop(0, H)
    def _(h):
        wide = jnp.broadcast_to(vec_v[pl.ds(h, 1), :], (128, vec_v.shape[1]))
        rolled = pltpu.roll(wide, vec_v.shape[1] - 127, 1, stride=1, stride_axis=0)
        toe_v[h] = rolled[:, : toe_v.shape[2]]


def attend(q_v, k_v, v_v, q0, k0, v0, mask_v, toe_v, s_v, p_v, mix_v, lse_v):
    length = mix_v.shape[0]

    @pl.loop(0, PAIRS)
    def _(hp):
        at = lambda base: pl.ds(pl.multiple_of(base + hp * 128, 128), 128)
        q2, k2, v2 = q_v[:, at(q0)], k_v[:, at(k0)], v_v[:, at(v0)]
        low = head_lanes(False)
        outs, tops = [], []
        for a in range(2):
            mine = head_lanes(a == 1)
            s_v[a] = mm_nt(jnp.where(mine, q2, jnp.zeros_like(q2)), k2)
            top = []
            for c in range(length // 128):
                rows = pl.ds(c * 128, 128)
                s = s_v[a, rows, :] + mask_v[rows, :]
                if toe_v is not None:
                    left = toe_v.shape[2] - length - c * 128
                    s = s + toe_v[2 * hp + a, :, left : left + length]
                m = jnp.max(s, axis=-1, keepdims=True)
                p_v[a, rows, :] = jnp.exp(s - m).astype(BF16)
                top.append(m)
            tops.append(jnp.concatenate(top, axis=0))
            outs.append(mm(p_v[a], jnp.where(mine, v2, jnp.ones_like(v2))))
        total = pltpu.roll(jnp.where(low, outs[1], outs[0]), HD, 1)
        mix_v[:, at(0)] = (jnp.where(low, outs[0], outs[1]) / total).astype(BF16)
        stat = (jnp.where(low, tops[0], tops[1]) + jnp.log(total)).T
        lse_v[pl.ds(2 * hp, 1), :] = stat[0:1, :]
        lse_v[pl.ds(2 * hp + 1, 1), :] = stat[HD : HD + 1, :]


def attend_back(q_v, k_v, v_v, dm_v, mix_v, q0, k0, v0, mask_v, toe_v, lse_v, dp_v, s_v, p_v, ds_v, out_v, o0, acc_v):
    length = mix_v.shape[0]

    @pl.loop(0, PAIRS)
    def _(hp):
        at = lambda base: pl.ds(pl.multiple_of(base + hp * 128, 128), 128)
        q2, k2, v2, dm2 = q_v[:, at(q0)], k_v[:, at(k0)], v_v[:, at(v0)], dm_v[:, at(0)]
        low = head_lanes(False)
        prod = (dm2.astype(F32) * mix_v[:, at(0)].astype(F32)).T
        k2t = k2.T
        dvs, dks, dqs = [], [], []
        for a in range(2):
            mine = head_lanes(a == 1)
            s_v[a] = mm_nt(jnp.where(mine, k2, jnp.zeros_like(k2)), q2)
            dp_v[a] = mm_nt(jnp.where(mine, v2, jnp.zeros_like(v2)), dm2)
            delta = jnp.sum(prod[a * HD : (a + 1) * HD, :], axis=0, keepdims=True)
            lse = lse_v[pl.ds(2 * hp + a, 1), :]
            for c in range(length // 128):
                rows = pl.ds(c * 128, 128)
                s = s_v[a, rows, :] + mask_v[rows, :]
                if toe_v is not None:
                    left = toe_v.shape[2] - length - c * 128
                    s = s + toe_v[2 * hp + a, :, left : left + length]
                p = jnp.exp(s - lse)
                p_v[a, rows, :] = p.astype(BF16)
                ds = p * (dp_v[a, rows, :] - delta)
                ds_v[a, rows, :] = ds.astype(BF16)
                if acc_v is not None:
                    acc_v[2 * hp + a, :, left : left + length] += ds
            dvs.append(mm(p_v[a], dm2))
            dks.append(mm(ds_v[a], q2))
            dqs.append(mm(k2t[a * HD : (a + 1) * HD, :], ds_v[a]))
        out_v[:, at(o0)] = jnp.concatenate(dqs, axis=0).T.astype(BF16)
        out_v[:, at(o0 + PAIRS * 128)] = jnp.where(low, dks[0], dks[1]).astype(BF16)
        out_v[:, at(o0 + 2 * PAIRS * 128)] = jnp.where(low, dvs[0], dvs[1]).astype(BF16)


def fold_diagonals(acc_v, diag_v, fold_v):
    extent = acc_v.shape[2]

    @pl.loop(0, H)
    def _(h):
        fold_v[:, :extent] = acc_v[h]
        fold_v[:, extent:] = jnp.zeros((128, fold_v.shape[1] - extent), F32)
        wide = fold_v.shape[1]
        half = 64
        value = fold_v[...]
        while half >= 1:
            upper, lower = value[:half], value[half:]
            value = pltpu.roll(upper, half, 1) + lower
            half //= 2
        diag_v[pl.ds(h, 1), :] = value


def gelu_parts(u):
    square = u * u
    bend = u * (GELU + (GELU * CUBIC) * square)
    half = 0.5 + 0.5 * jnp.tanh(bend)
    hidden = u * half
    slope = half + 2.0 * hidden * (1.0 - half) * (GELU + (3.0 * GELU * CUBIC) * square)
    return hidden, slope


def ffn_up(n_v, win_v, h_v, slope_v):
    tile = 512

    @pl.loop(0, win_v.shape[1] // tile)
    def _(t):
        cols = pl.ds(pl.multiple_of(t * tile, tile), tile)
        hidden, slope = gelu_parts(mm(n_v[...], win_v[:, cols]))
        h_v[:, cols] = hidden.astype(BF16)
        slope_v[:, cols] = slope.astype(BF16)


def rows_out(a_v, w_v, w0, out_v, add):
    tile = 256
    depth = a_v.shape[1]

    @pl.loop(0, w_v.shape[0] // tile)
    def _(t):
        cols = pl.ds(pl.multiple_of(t * tile, tile), tile)
        part = mm_nt(a_v[...], w_v[cols, w0 : w0 + depth])
        if add:
            out_v[:, cols] = out_v[:, cols] + part
        else:
            out_v[:, cols] = part.astype(out_v.dtype)


def ffn_down(d_v, wout_v, slope_v, du_v):
    tile = 512

    @pl.loop(0, wout_v.shape[1] // tile)
    def _(t):
        cols = pl.ds(pl.multiple_of(t * tile, tile), tile)
        grad = mm(d_v[...], wout_v[:, cols])
        du_v[:, cols] = (grad * slope_v[:, cols].astype(F32)).astype(BF16)


def project(a_v, w_v, w0, out_v, o0, width):
    tile = 384

    @pl.loop(0, width // tile)
    def _(t):
        source = pl.ds(pl.multiple_of(w0 + t * tile, 128), tile)
        target = pl.ds(pl.multiple_of(o0 + t * tile, 128), tile)
        out_v[:, target] = mm(a_v[...], w_v[:, source]).astype(out_v.dtype)


def flops_of(matmuls, size):
    return pl.CostEstimate(flops=matmuls * 2 * 512 * 768 * 3072, bytes_accessed=size, transcendentals=0)


def call(kernel, outs, scratch, ins, in_vmem, cost):
    spec = lambda small: pl.BlockSpec(memory_space=pltpu.VMEM if small else pl.ANY)
    return pl.pallas_call(
        kernel,
        out_shape=outs,
        in_specs=[spec(small) for small in in_vmem],
        out_specs=[spec(False) for _ in outs],
        scratch_shapes=scratch,
        compiler_params=pltpu.CompilerParams(vmem_limit_bytes=VMEM_LIMIT),
        cost_estimate=cost,
    )(*ins)


def shape(dims, kind):
    return jax.ShapeDtypeStruct(dims, kind)


def self_forward(row, ins, mats, gains, segs, tables, buckets):
    length, width = segs.shape[1], ins.shape[1]
    dist = 2 * length

    def kernel(x_h, w_h, gain_r, seg_r, table_r, bucket_r, e_h, n_h, qkv_h, mix_h, lse_h,
               x_v, w_v, n_v, qkv_v, mix_v, lse_v, e_v, mask_v, toe_v, vec_v, s_v, p_v, sems):
        section = lax.axis_index("section")

        @pl.when(section % 2 == 0)
        def _():
            side = section // 2
            loads = copy_all(
                sems, 0,
                (x_h.at[pl.ds(row * length, length)], x_v),
                *[(w_h.at[0, :, pl.ds(c * width, width)], w_v.at[:, pl.ds(c * width, width)]) for c in range(4)],
            )
            fill_mask(mask_v, seg_r[row : row + 1, :], False, jnp.where(section == 2, 0, 2 * length))
            fill_toeplitz(toe_v, vec_v, table_r[side], bucket_r[pl.ds(side, 1), :])
            gain = gain_r[pl.ds(3 * side, 1), :]
            loads[0].wait()
            for rows in row_chunks(length):
                x = x_v[rows, :].astype(F32)
                n_v[rows, :] = (x * inverse_rms(x) * gain).astype(BF16)
            stores = copy_all(sems, 5, (n_v, n_h))
            wait_all(loads[1:4])
            project(n_v, w_v, 0, qkv_v, 0, 3 * width)
            stores += copy_all(sems, 6, (qkv_v, qkv_h))
            attend(qkv_v, qkv_v, qkv_v, 0, width, 2 * width, mask_v, toe_v, s_v, p_v, mix_v, lse_v)
            stores += copy_all(sems, 7, (mix_v, mix_h), (lse_v, lse_h))
            loads[4].wait()

            @pl.loop(0, width // 256)
            def _(t):
                cols = pl.ds(pl.multiple_of(t * 256, 256), 256)
                part = mm(mix_v[...], w_v[:, pl.ds(pl.multiple_of(3 * width + t * 256, 256), 256)])
                e_v[:, cols] = (x_v[:, cols].astype(F32) + part).astype(BF16)

            stores += copy_all(sems, 9, (e_v, e_h))
            wait_all(stores)

    return call(
        kernel,
        [
            shape((length, width), BF16),
            shape((length, width), BF16),
            shape((length, 3 * width), BF16),
            shape((length, width), BF16),
            shape((16, length), F32),
        ],
        [
            pltpu.VMEM((length, width), BF16),
            pltpu.VMEM((width, 4 * width), BF16),
            pltpu.VMEM((length, width), BF16),
            pltpu.VMEM((length, 3 * width), BF16),
            pltpu.VMEM((length, width), BF16),
            pltpu.VMEM((16, length), F32),
            pltpu.VMEM((length, width), BF16),
            pltpu.VMEM((length, length), F32),
            pltpu.VMEM((H, 128, 2 * length - 128), F32),
            pltpu.VMEM((16, dist), F32),
            pltpu.VMEM((2, length, length), F32),
            pltpu.VMEM((2, length, length), BF16),
            pltpu.SemaphoreType.DMA((10,)),
        ],
        [ins, mats, gains, segs, tables, buckets],
        [False, False, True, True, True, True],
        flops_of(3, 12 << 20),
    )


def self_backward(first, ins, mats, gains, segs, tables, flipped, g_enc, g_dec, kept):
    length, width = segs.shape[1], ins.shape[1]
    dist = 2 * length

    def kernel(x_h, w_h, gain_r, seg_r, table_r, bucket_r, ge_h, gd_h, n0_h, qkv0_h, mix0_h, lse0_h,
               n1_h, qkv1_h, mix1_h, lse1_h, gx_h, dgain_h, diag_h, a_h, b_h,
               x_v, w_v, qkv_v, mix_v, lse_v, d_v, dm_v, dqkv_v, dn_v, gx_v, dgain_v, diag_v,
               mask_v, toe_v, acc_v, vec_v, fold_v, s_v, dp_v, p_v, ds_v, sems):
        section = lax.axis_index("section")

        def run(side, row, g_h, n_h, qkv_h, mix_h, lse_h):
            loads = copy_all(
                sems, 0,
                (g_h, d_v),
                (w_h.at[0, :, pl.ds(3 * width, width)], w_v.at[:, pl.ds(3 * width, width)]),
                (mix_h, mix_v),
                (lse_h, lse_v),
                (qkv_h, qkv_v),
                (w_h.at[0, :, pl.ds(0, 3 * width)], w_v.at[:, pl.ds(0, 3 * width)]),
                (x_h.at[pl.ds(row * length, length)], x_v),
            )
            through = copy_all(
                sems, 7,
                (n_h, a_h.at[:, pl.ds(0, width)]),
                (mix_h, a_h.at[:, pl.ds(width, width)]),
                (g_h, b_h.at[:, pl.ds(3 * width, width)]),
            )
            fill_mask(mask_v, seg_r[row : row + 1, :], True, 0 if side else 2 * length)
            fill_toeplitz(toe_v, vec_v, table_r[side], bucket_r[side : side + 1, :])
            acc_v[...] = jnp.zeros_like(acc_v)
            gain = gain_r[3 * side : 3 * side + 1, :]
            wait_all(loads[:2])
            rows_out(d_v, w_v, 3 * width, dm_v, False)
            wait_all(loads[2:5])
            attend_back(qkv_v, qkv_v, qkv_v, dm_v, mix_v, 0, width, 2 * width, mask_v, toe_v, lse_v,
                        dp_v, s_v, p_v, ds_v, dqkv_v, 0, acc_v)
            stores = copy_all(sems, 10, (dqkv_v, b_h.at[:, pl.ds(0, 3 * width)]))
            wait_all(loads[5:])
            rows_out(dqkv_v, w_v, 0, dn_v, False)
            total = jnp.zeros((1, width), F32)
            for rows in row_chunks(length):
                dx, dgain = rms_back(x_v[rows, :].astype(F32), gain, dn_v[rows, :])
                gx_v[rows, :] = d_v[rows, :].astype(F32) + dx
                total = total + dgain
            dgain_v[...] = total
            stores += copy_all(sems, 11, (gx_v, gx_h), (dgain_v, dgain_h))
            fold_diagonals(acc_v, diag_v, fold_v)
            stores += copy_all(sems, 13, (diag_v, diag_h))
            wait_all(through)
            wait_all(stores)

        @pl.when(section == 0)
        def _():
            kept_refs = (n0_h, qkv0_h, mix0_h, lse0_h) if first else (n1_h, qkv1_h, mix1_h, lse1_h)
            run(0, 0 if first else 1, ge_h, *kept_refs)

        @pl.when(section == 2)
        def _():
            kept_refs = (n1_h, qkv1_h, mix1_h, lse1_h) if first else (n0_h, qkv0_h, mix0_h, lse0_h)
            run(1, 1 if first else 0, gd_h, *kept_refs)

    kept0, kept1 = kept
    return call(
        kernel,
        [
            shape((length, width), F32),
            shape((1, width), F32),
            shape((16, dist), F32),
            shape((length, 2 * width), BF16),
            shape((length, 4 * width), BF16),
        ],
        [
            pltpu.VMEM((length, width), BF16),
            pltpu.VMEM((width, 4 * width), BF16),
            pltpu.VMEM((length, 3 * width), BF16),
            pltpu.VMEM((length, width), BF16),
            pltpu.VMEM((16, length), F32),
            pltpu.VMEM((length, width), BF16),
            pltpu.VMEM((length, width), BF16),
            pltpu.VMEM((length, 3 * width), BF16),
            pltpu.VMEM((length, width), F32),
            pltpu.VMEM((length, width), F32),
            pltpu.VMEM((1, width), F32),
            pltpu.VMEM((16, dist), F32),
            pltpu.VMEM((length, length), F32),
            pltpu.VMEM((H, 128, dist - 128), F32),
            pltpu.VMEM((H, 128, dist - 128), F32),
            pltpu.VMEM((16, dist), F32),
            pltpu.VMEM((128, dist), F32),
            pltpu.VMEM((2, length, length), F32),
            pltpu.VMEM((2, length, length), F32),
            pltpu.VMEM((2, length, length), BF16),
            pltpu.VMEM((2, length, length), BF16),
            pltpu.SemaphoreType.DMA((14,)),
        ],
        [ins, mats, gains, segs, tables, flipped, g_enc, g_dec, *kept0, *kept1],
        [False, False, True, True, True, True] + [False] * 10,
        flops_of(6, 16 << 20),
    )


def encoder_forward(e1, mats, gains):
    length, width = e1.shape
    hidden = mats.shape[2]

    def kernel(e_h, w_h, gain_r, out_h, send_h, mid_h, n_h, h_h, slope_h,
               e_v, win_v, wout_v, n_v, h_v, slope_v, mid_v, out_v, send_v, sems):
        @pl.when(lax.axis_index("section") == 1)
        def _():
            loads = copy_all(sems, 0, (e_h, e_v), (w_h.at[0], win_v), (w_h.at[1], wout_v))
            loads[0].wait()
            for rows in row_chunks(length):
                x = e_v[rows, :].astype(F32)
                mid_v[rows, :] = x
                n_v[rows, :] = (x * inverse_rms(x) * gain_r[1:2, :]).astype(BF16)
            stores = copy_all(sems, 3, (n_v, n_h))
            loads[1].wait()
            ffn_up(n_v, win_v, h_v, slope_v)
            stores += copy_all(sems, 4, (h_v, h_h), (slope_v, slope_h))
            loads[2].wait()
            rows_out(h_v, wout_v, 0, mid_v, True)
            for rows in row_chunks(length):
                x = mid_v[rows, :]
                y = x * inverse_rms(x) * gain_r[2:3, :]
                out_v[rows, :] = y
                send_v[rows, :] = y.astype(BF16)
            stores += copy_all(sems, 6, (send_v, send_h), (out_v, out_h), (mid_v, mid_h))
            wait_all(stores)

    return call(
        kernel,
        [
            shape((length, width), F32),
            shape((length, width), BF16),
            shape((length, width), F32),
            shape((length, width), BF16),
            shape((length, hidden), BF16),
            shape((length, hidden), BF16),
        ],
        [
            pltpu.VMEM((length, width), BF16),
            pltpu.VMEM((width, hidden), BF16),
            pltpu.VMEM((width, hidden), BF16),
            pltpu.VMEM((length, width), BF16),
            pltpu.VMEM((length, hidden), BF16),
            pltpu.VMEM((length, hidden), BF16),
            pltpu.VMEM((length, width), F32),
            pltpu.VMEM((length, width), F32),
            pltpu.VMEM((length, width), BF16),
            pltpu.SemaphoreType.DMA((9,)),
        ],
        [e1, mats, gains],
        [False, False, True],
        flops_of(2, 20 << 20),
    )


def encoder_backward(row, ins, extra, e1, mid, slope, mats, gains):
    length, width = e1.shape
    hidden = mats.shape[2]

    def kernel(cot_h, extra_h, e_h, mid_h, slope_h, w_h, gain_r, g_h, d_h, du_h, dgain_h,
               cot_v, extra_v, e_v, mid_v, slope_v, win_v, wout_v, d_v, du_v, dn_v, gm_v, g_v, dgain_v, sems):
        @pl.when(lax.axis_index("section") == 1)
        def _():
            loads = copy_all(
                sems, 0,
                (cot_h.at[pl.ds(row * length, length)], cot_v), (extra_h, extra_v), (mid_h, mid_v),
                (w_h.at[1], wout_v), (slope_h, slope_v), (w_h.at[0], win_v), (e_h, e_v),
            )
            wait_all(loads[:3])
            total = jnp.zeros((1, width), F32)
            for rows in row_chunks(length):
                dy = cot_v[rows, :].astype(F32) + extra_v[rows, :].astype(F32)
                dx, dgain = rms_back(mid_v[rows, :], gain_r[2:3, :], dy)
                gm_v[rows, :] = dx
                d_v[rows, :] = dx.astype(BF16)
                total = total + dgain
            dgain_v[1:2, :] = total
            stores = copy_all(sems, 7, (d_v, d_h))
            wait_all(loads[3:5])
            ffn_down(d_v, wout_v, slope_v, du_v)
            stores += copy_all(sems, 8, (du_v, du_h))
            wait_all(loads[5:])
            rows_out(du_v, win_v, 0, dn_v, False)
            total = jnp.zeros((1, width), F32)
            for rows in row_chunks(length):
                dx, dgain = rms_back(e_v[rows, :].astype(F32), gain_r[1:2, :], dn_v[rows, :])
                g_v[rows, :] = (gm_v[rows, :] + dx).astype(BF16)
                total = total + dgain
            dgain_v[0:1, :] = total
            stores += copy_all(sems, 9, (g_v, g_h), (dgain_v, dgain_h))
            wait_all(stores)

    return call(
        kernel,
        [
            shape((length, width), BF16),
            shape((length, width), BF16),
            shape((length, hidden), BF16),
            shape((2, width), F32),
        ],
        [
            pltpu.VMEM((length, width), BF16),
            pltpu.VMEM((length, width), BF16),
            pltpu.VMEM((length, width), BF16),
            pltpu.VMEM((length, width), F32),
            pltpu.VMEM((length, hidden), BF16),
            pltpu.VMEM((width, hidden), BF16),
            pltpu.VMEM((width, hidden), BF16),
            pltpu.VMEM((length, width), BF16),
            pltpu.VMEM((length, hidden), BF16),
            pltpu.VMEM((length, width), F32),
            pltpu.VMEM((length, width), F32),
            pltpu.VMEM((length, width), BF16),
            pltpu.VMEM((2, width), F32),
            pltpu.SemaphoreType.DMA((11,)),
        ],
        [ins, extra, e1, mid, slope, mats, gains],
        [False] * 6 + [True],
        flops_of(2, 20 << 20),
    )


def decoder_forward(d_own, d_got, m_three, m_two, ins, cot_got, mats, got_mats, gains, segs):
    length, width = d_own.shape
    hidden = mats.shape[2]
    wa, wb, wc = got_mats

    def kernel(d2_h, d3_h, m3_h, m2_h, c3_h, c2_h, w_h, wa_h, wb_h, wc_h, gain_r, seg_r,
               out_h, gc_h, q_h, mix_h, lse_h, n4_h, ka_h, kb_h, sa_h, sb_h, dgain_h,
               d_v, m_v, c_v, wca_v, win_v, wout_v, n_v, q_v, mix_v, lse_v, mask_v, s_v, p_v, h_v, slope_v,
               x_v, y_v, dn_v, n5_v, do_v, dgain_v, sems):
        section = lax.axis_index("section")

        def run(row, d_h, m_h, c_h, matrices, na_h, nb_h, oa_h, ob_h):
            loads = copy_all(
                sems, 0,
                (d_h, d_v), (m_h, m_v), (matrices[0], wca_v), (matrices[1], win_v), (matrices[2], wout_v), (c_h, c_v),
            )
            fill_mask(mask_v, seg_r[row : row + 1, :], False, 2 * length)
            loads[0].wait()
            for rows in row_chunks(length):
                x = d_v[rows, :].astype(F32)
                x_v[rows, :] = x
                n_v[rows, :] = (x * inverse_rms(x) * gain_r[4:5, :]).astype(BF16)
            stores = copy_all(sems, 6, (n_v, n4_h))
            wait_all(loads[1:3])
            project(n_v, wca_v, 0, q_v, 0, width)
            project(m_v, wca_v, width, q_v, width, 2 * width)
            stores += copy_all(sems, 7, (q_v, q_h))
            attend(q_v, q_v, q_v, 0, width, 2 * width, mask_v, None, s_v, p_v, mix_v, lse_v)
            stores += copy_all(sems, 8, (mix_v, mix_h), (lse_v, lse_h))

            @pl.loop(0, width // 256)
            def _(t):
                cols = pl.ds(pl.multiple_of(t * 256, 256), 256)
                part = mm(mix_v[...], wca_v[:, pl.ds(pl.multiple_of(3 * width + t * 256, 256), 256)])
                x_v[:, cols] = x_v[:, cols] + part

            for rows in row_chunks(length):
                x = x_v[rows, :]
                y_v[rows, :] = x
                n5_v[rows, :] = (x * inverse_rms(x) * gain_r[5:6, :]).astype(BF16)
            stores += copy_all(sems, 10, (n5_v, na_h))
            loads[3].wait()
            ffn_up(n5_v, win_v, h_v, slope_v)
            stores += copy_all(sems, 11, (h_v, ob_h))
            loads[4].wait()
            rows_out(h_v, wout_v, 0, y_v, True)
            loads[5].wait()
            total = jnp.zeros((1, width), F32)
            for rows in row_chunks(length):
                y = y_v[rows, :]
                dn_v[rows, :] = y * inverse_rms(y) * gain_r[6:7, :]
                dy, dgain = rms_back(y, gain_r[6:7, :], c_v[rows, :].astype(F32))
                total = total + dgain
                do_v[rows, :] = dy.astype(BF16)
                y_v[rows, :] = dy
            dgain_v[1:2, :] = total
            last = copy_all(sems, 12, (dn_v, out_h))
            stores += copy_all(sems, 13, (do_v, oa_h))
            ffn_down(do_v, wout_v, slope_v, slope_v)
            stores += copy_all(sems, 14, (slope_v, nb_h))
            wait_all(last)
            rows_out(slope_v, win_v, 0, dn_v, False)
            total = jnp.zeros((1, width), F32)
            for rows in row_chunks(length):
                dx, dgain = rms_back(x_v[rows, :], gain_r[5:6, :], dn_v[rows, :])
                y_v[rows, :] = y_v[rows, :] + dx
                total = total + dgain
            dgain_v[0:1, :] = total
            stores += copy_all(sems, 15, (y_v, gc_h), (dgain_v, dgain_h))
            wait_all(stores)

        @pl.when(section == 3)
        def _():
            run(0, d3_h, m3_h, c3_h.at[pl.ds(0, length)], (w_h.at[0], w_h.at[1], w_h.at[2]), ka_h, kb_h, sa_h, sb_h)

        @pl.when(section == 2)
        def _():
            run(1, d2_h, m2_h, c2_h, (wa_h, wb_h, wc_h), sa_h, sb_h, ka_h, kb_h)

    return call(
        kernel,
        [
            shape((length, width), F32),
            shape((length, width), F32),
            shape((length, 3 * width), BF16),
            shape((length, width), BF16),
            shape((16, length), F32),
            shape((length, width), BF16),
            shape((length, width), BF16),
            shape((length, hidden), BF16),
            shape((length, width), BF16),
            shape((length, hidden), BF16),
            shape((2, width), F32),
        ],
        [
            pltpu.VMEM((length, width), BF16),
            pltpu.VMEM((length, width), BF16),
            pltpu.VMEM((length, width), BF16),
            pltpu.VMEM((width, 4 * width), BF16),
            pltpu.VMEM((width, hidden), BF16),
            pltpu.VMEM((width, hidden), BF16),
            pltpu.VMEM((length, width), BF16),
            pltpu.VMEM((length, 3 * width), BF16),
            pltpu.VMEM((length, width), BF16),
            pltpu.VMEM((16, length), F32),
            pltpu.VMEM((length, length), F32),
            pltpu.VMEM((2, length, length), F32),
            pltpu.VMEM((2, length, length), BF16),
            pltpu.VMEM((length, hidden), BF16),
            pltpu.VMEM((length, hidden), BF16),
            pltpu.VMEM((length, width), F32),
            pltpu.VMEM((length, width), F32),
            pltpu.VMEM((length, width), F32),
            pltpu.VMEM((length, width), BF16),
            pltpu.VMEM((length, width), BF16),
            pltpu.VMEM((2, width), F32),
            pltpu.SemaphoreType.DMA((17,)),
        ],
        [d_own, d_got, m_three, m_two, ins, cot_got, mats, wa, wb, wc, gains, segs],
        [False] * 10 + [True, True],
        flops_of(7, 30 << 20),
    )


def decoder_backward(d_own, d_got, m_three, m_two, kept, mats, got_mats, gains, segs):
    length, width = d_own.shape
    gc, q, mix, lse, n4 = kept

    def kernel(d2_h, d3_h, m3_h, m2_h, gc_h, q_h, mix_h, lse_h, n4_h, w_h, wa_h, gain_r, seg_r,
               gm_h, gd_h, ka_h, kb_h, sa_h, sb_h, dgain_h,
               d_v, gc_v, q_v, mix_v, lse_v, w_v, do_v, dm_v, dq_v, dn_v, gm_v, gd_v, dgain_v,
               mask_v, s_v, dp_v, p_v, ds_v, sems):
        section = lax.axis_index("section")

        def run(row, d_h, m_h, matrix, fa_h, fb_h, la_h, lb_h):
            left, right = pl.ds(0, width), pl.ds(width, width)
            loads = copy_all(
                sems, 0,
                (gc_h, gc_v), (matrix, w_v), (mix_h, mix_v), (lse_h, lse_v), (q_h, q_v), (d_h, d_v),
            )
            through = copy_all(
                sems, 6,
                (n4_h, fa_h.at[:, left]), (m_h, fa_h.at[:, right]), (m_h, la_h.at[:, left]), (mix_h, la_h.at[:, right]),
            )
            fill_mask(mask_v, seg_r[row : row + 1, :], True, 2 * length)
            loads[0].wait()
            for rows in row_chunks(length):
                do_v[rows, :] = gc_v[rows, :].astype(BF16)
            stores = copy_all(sems, 10, (do_v, lb_h.at[:, right]))
            loads[1].wait()
            rows_out(do_v, w_v, 3 * width, dm_v, False)
            wait_all(loads[2:5])
            attend_back(q_v, q_v, q_v, dm_v, mix_v, 0, width, 2 * width, mask_v, None, lse_v,
                        dp_v, s_v, p_v, ds_v, dq_v, 0, None)
            stores += copy_all(
                sems, 11,
                (dq_v.at[:, pl.ds(0, 2 * width)], fb_h), (dq_v.at[:, pl.ds(2 * width, width)], lb_h.at[:, left]),
            )
            rows_out(dq_v.at[:, width:], w_v, width, gm_v, False)
            stores += copy_all(sems, 13, (gm_v, gm_h))
            rows_out(dq_v.at[:, :width], w_v, 0, dn_v, False)
            loads[5].wait()
            total = jnp.zeros((1, width), F32)
            for rows in row_chunks(length):
                dx, dgain = rms_back(d_v[rows, :].astype(F32), gain_r[4:5, :], dn_v[rows, :])
                gd_v[rows, :] = (gc_v[rows, :] + dx).astype(BF16)
                total = total + dgain
            dgain_v[...] = total
            stores += copy_all(sems, 14, (gd_v, gd_h), (dgain_v, dgain_h))
            wait_all(through)
            wait_all(stores)

        @pl.when(section == 3)
        def _():
            run(0, d3_h, m3_h, w_h.at[0], ka_h, kb_h, sa_h, sb_h)

        @pl.when(section == 2)
        def _():
            run(1, d2_h, m2_h, wa_h, sa_h, sb_h, ka_h, kb_h)

    return call(
        kernel,
        [
            shape((length, width), BF16),
            shape((length, width), BF16),
            shape((length, 2 * width), BF16),
            shape((length, 2 * width), BF16),
            shape((length, 2 * width), BF16),
            shape((length, 2 * width), BF16),
            shape((1, width), F32),
        ],
        [
            pltpu.VMEM((length, width), BF16),
            pltpu.VMEM((length, width), F32),
            pltpu.VMEM((length, 3 * width), BF16),
            pltpu.VMEM((length, width), BF16),
            pltpu.VMEM((16, length), F32),
            pltpu.VMEM((width, 4 * width), BF16),
            pltpu.VMEM((length, width), BF16),
            pltpu.VMEM((length, width), BF16),
            pltpu.VMEM((length, 3 * width), BF16),
            pltpu.VMEM((length, width), F32),
            pltpu.VMEM((length, width), BF16),
            pltpu.VMEM((length, width), BF16),
            pltpu.VMEM((1, width), F32),
            pltpu.VMEM((length, length), F32),
            pltpu.VMEM((2, length, length), F32),
            pltpu.VMEM((2, length, length), F32),
            pltpu.VMEM((2, length, length), BF16),
            pltpu.VMEM((2, length, length), BF16),
            pltpu.SemaphoreType.DMA((16,)),
        ],
        [d_own, d_got, m_three, m_two, gc, q, mix, lse, n4, mats, got_mats[0], gains, segs],
        [False] * 11 + [True, True],
        flops_of(5, 16 << 20),
    )


def weight_grad(sections, groups, ndp):
    length, width = groups[0][0][0][0].shape[0], 768
    columns = sum(group[2] for group in groups)
    pieces = len(groups[0][0])
    bits = ndp.bit_length() - 1
    block = width // ndp
    refs, flat = [], []
    for a_list, b_list, _ in groups:
        for array, _ in a_list + b_list:
            if not any(array is other for other in flat):
                flat.append(array)
    place = lambda array: [index for index, other in enumerate(flat) if other is array][0]
    plan = [
        ([(place(a), a0) for a, a0 in a_list], [(place(b), b0) for b, b0 in b_list], count)
        for a_list, b_list, count in groups
    ]
    tile = 384 if columns % 384 == 0 else 256
    copies = 2 * pieces * len(groups)

    def kernel(*args):
        sources = args[: len(flat)]
        keep_h, send_h, a_v, at_v, b_v, out_v, sems = args[len(flat) :]
        me = lax.axis_index("dp")
        section = lax.axis_index("section")
        active = section == sections[0]
        for other in sections[1:]:
            active = active | (section == other)

        @pl.when(active)
        def _():
            loads, start = [], 0
            for g, (a_list, b_list, count) in enumerate(plan):
                group_loads = []
                for k in range(pieces):
                    rows = pl.ds(k * length, length)
                    (ai, a0), (bi, b0) = a_list[k], b_list[k]
                    group_loads += copy_all(
                        sems, 2 * (g * pieces + k),
                        (sources[ai].at[:, pl.ds(a0, width)], a_v.at[g, rows]),
                        (sources[bi].at[:, pl.ds(b0, count)], b_v.at[rows, pl.ds(start, count)]),
                    )
                loads.append(group_loads)
                start += count
            spots = []
            for b in range(ndp):
                code = jnp.bitwise_xor(me, b)
                spot = 0
                for k in range(bits):
                    spot = spot + ((code >> k) & 1) * (1 << (bits - 1 - k))
                spots.append(spot)
            start = 0
            for g, (_, _, count) in enumerate(plan):
                wait_all(loads[g])
                at_v[...] = a_v[g].T

                @pl.loop(0, count // tile)
                def _(t):
                    cols = pl.ds(pl.multiple_of(start + t * tile, 128), tile)
                    part = mm(at_v[...], b_v[:, cols])
                    for b in range(ndp):
                        out_v[spots[b], :, cols] = part[b * block : (b + 1) * block, :].astype(BF16)

                start += count
            wait_all(
                copy_all(
                    sems, copies,
                    (out_v.at[pl.ds(0, ndp // 2)], keep_h), (out_v.at[pl.ds(ndp // 2, ndp // 2)], send_h),
                )
            )

    return call(
        kernel,
        [shape((ndp // 2, block, columns), BF16)] * 2,
        [
            pltpu.VMEM((len(groups), pieces * length, width), BF16),
            pltpu.VMEM((width, pieces * length), BF16),
            pltpu.VMEM((pieces * length, columns), BF16),
            pltpu.VMEM((ndp, block, columns), BF16),
            pltpu.SemaphoreType.DMA((copies + 2,)),
        ],
        flat,
        [False] * len(flat),
        flops_of(2 * columns // 3072 or 1, 14 << 20),
    )


def along_dp(value, bit, sections, ndp):
    pairs = [(s * ndp + d, s * ndp + (d ^ bit)) for s in sections for d in range(ndp)]
    return lax.ppermute(value, ("section", "dp"), pairs)


def sum_shards(halves, sections, ndp):
    keep, send = halves
    bit = 1
    while True:
        got = along_dp(send, bit, sections, ndp)
        total = keep.astype(F32) + got.astype(F32)
        half = keep.shape[0] // 2
        if half == 0:
            return total[0]
        keep, send = total[:half].astype(BF16), total[half:].astype(BF16)
        bit *= 2


def per_device(section_ins, segments, buckets, section_mats, gains, tables):
    section = lax.axis_index("section")
    ndp = lax.axis_size("dp")
    ins = section_ins[0]
    mats = section_mats[0]
    rows, length = segments.shape
    width = ins.shape[1]
    segs = segments.astype(F32)
    flat_tables = jnp.pad(jnp.swapaxes(tables, 1, 2), ((0, 0), (0, 16 - H), (0, 0)))
    flipped = buckets[:, ::-1]
    move = lambda value, pairs: lax.ppermute(value, "section", pairs)

    got_mats = tuple(move(mats[slot], [(3, 2)]) for slot in range(3))
    cot_got = move(ins[length:], [(3, 2)])

    fwd0 = self_forward(0, ins, mats, gains, segs, flat_tables, buckets)
    first0 = move(fwd0[0], [(0, 1), (2, 3)])
    fwd1 = self_forward(1, ins, mats, gains, segs, flat_tables, buckets)
    first1 = move(fwd1[0], [(0, 1)])
    enc0 = encoder_forward(first0, mats, gains)
    m_three = move(enc0[1], [(1, 3)])
    enc1 = encoder_forward(first1, mats, gains)
    m_two = move(enc1[1], [(1, 2)])

    dec = decoder_forward(fwd1[0], first0, m_three, m_two, ins, cot_got, mats, got_mats, gains, segs)
    out_dec, gc, q, mix, lse, n4, keep_a, keep_b, send_a, send_b, dgain_d = dec
    got_a, got_b = move(send_a, [(2, 3), (3, 2)]), move(send_b, [(2, 3), (3, 2)])
    out_got = move(out_dec, [(2, 3)])
    back = decoder_backward(fwd1[0], first0, m_three, m_two, (gc, q, mix, lse, n4), mats, got_mats, gains, segs)
    g_mem, g_dec, ca_keep_a, ca_keep_b, ca_send_a, ca_send_b, dgain_c = back
    extra0 = move(g_mem, [(3, 1)])
    extra1 = move(g_mem, [(2, 1)])
    g_dec_got = move(g_dec, [(3, 2)])
    ca_got_a, ca_got_b = move(ca_send_a, [(2, 3), (3, 2)]), move(ca_send_b, [(2, 3), (3, 2)])

    halves = weight_grad((2, 3), [([(keep_a, 0), (got_a, 0)], [(keep_b, 0), (got_b, 0)], 4 * width)], ndp)
    shard_ffn = sum_shards(halves, (2, 3), ndp)

    bwd0 = encoder_backward(0, ins, extra0, first0, enc0[2], enc0[5], mats, gains)
    g0 = move(bwd0[0], [(1, 0)])
    halves = weight_grad(
        (2, 3),
        [
            ([(ca_keep_a, c), (ca_got_a, c)], [(ca_keep_b, c), (ca_got_b, c)], width)
            for c in (0, width)
        ],
        ndp,
    )
    shard_ca = sum_shards(halves, (2, 3), ndp)

    kept = (fwd0[1:], fwd1[1:])
    self_a = self_backward(True, ins, mats, gains, segs, flat_tables, flipped, g0, g_dec, kept)
    bwd1 = encoder_backward(1, ins, extra1, first1, enc1[2], enc1[5], mats, gains)
    g1 = move(bwd1[0], [(1, 0)])
    halves = weight_grad((1,), [([(enc0[3], 0), (enc1[3], 0)], [(bwd0[2], 0), (bwd1[2], 0)], 4 * width)], ndp)
    shard_in = sum_shards(halves, (1,), ndp)
    halves = weight_grad((1,), [([(bwd0[1], 0), (bwd1[1], 0)], [(enc0[4], 0), (enc1[4], 0)], 4 * width)], ndp)
    shard_out = sum_shards(halves, (1,), ndp)
    self_b = self_backward(False, ins, mats, gains, segs, flat_tables, flipped, g1, g_dec_got, kept)
    halves = weight_grad(
        (0, 2),
        [
            ([(self_a[3], 0), (self_b[3], 0)], [(self_a[4], 0), (self_b[4], 0)], 3 * width),
            ([(self_a[3], width), (self_b[3], width)], [(self_a[4], 3 * width), (self_b[4], 3 * width)], width),
        ],
        ndp,
    )
    shard_self = sum_shards(halves, (0, 2), ndp)

    def only(flag, value):
        return jnp.where(flag, value, jnp.zeros_like(value))

    on_self = section % 2 == 0
    self_gain = only(on_self, self_a[1] + self_b[1])
    enc_gain = only(section == 1, bwd0[3] + bwd1[3])
    cross_gain = only(section >= 2, dgain_c)
    ffn_gain = only(section >= 2, dgain_d)
    part_gain = jnp.concatenate(
        [
            only(section == 0, self_gain),
            enc_gain,
            only(section == 2, self_gain),
            cross_gain,
            ffn_gain,
        ],
        axis=0,
    )
    diag = only(on_self, self_a[2] + self_b[2])[:H]
    side = section // 2
    own_buckets = flipped[side]
    onehot = (own_buckets[:, None] == jnp.arange(tables.shape[1], dtype=jnp.int32)[None, :]).astype(F32)
    table_part = jnp.dot(diag[:, : own_buckets.shape[0]], onehot, precision=lax.Precision.HIGHEST).T
    sides = jnp.arange(tables.shape[0], dtype=jnp.int32)[:, None, None]
    part_table = jnp.where(sides == side, table_part[None], 0.0)
    small = jnp.concatenate([part_gain.reshape(-1, 128), part_table.reshape(-1, 128)], axis=0)
    everyone = lax.axis_size("section") * ndp
    bit = 1
    while bit < everyone:
        small = small + lax.ppermute(small, ("section", "dp"), [(d, d ^ bit) for d in range(everyone)])
        bit *= 2
    cut = gains.size // 128
    gains_grad = small[:cut].reshape(gains.shape)
    tables_grad = small[cut:].reshape(tables.shape)

    three = move(jnp.concatenate([shard_ffn, shard_ca], axis=1).astype(BF16), [(2, 3)]).astype(F32)
    ffn_got, ca_got = three[:, : 4 * width], three[:, 4 * width :]
    zero = jnp.zeros_like(shard_self)
    full_ca = jnp.concatenate([shard_ca, ca_got], axis=1)
    pick = lambda own, enc, dec: jnp.where(on_self, own, jnp.where(section == 1, enc, dec))
    mats_grad = jnp.stack(
        [pick(shard_self, shard_in, full_ca), pick(zero, shard_out, shard_ffn), pick(zero, zero, ffn_got)]
    )
    row0 = jnp.where(section == 0, self_a[0], jnp.where(section == 1, enc0[0], jnp.where(section == 2, self_b[0], out_dec)))
    row1 = jnp.where(section == 0, self_b[0], jnp.where(section == 1, enc1[0], jnp.where(section == 2, self_a[0], out_got)))
    return jnp.concatenate([row0, row1], axis=0)[None], mats_grad[None], gains_grad, tables_grad


def solution(mesh):
    placed = (
        P("section", "dp", None),
        P("dp", None),
        P(),
        P("section", None, None, None),
        P(),
        P(),
    )
    return jax.shard_map(
        per_device,
        mesh=mesh,
        in_specs=placed,
        out_specs=(P("section", "dp", None), P("section", None, "dp", None), P(), P()),
        check_vma=False,
    )
```

time: 1390 us -> 621 us (0.45)
  local copies, waits for them, and re-layouts: 569 us -> 18.1 us
  Pallas kernels: 0 us -> 363 us
  blocking collectives: 199 us -> 0 us
  other arithmetic: 155 us -> 20 us
  matrix products: 123 us -> 1.43 us
  waiting for transfers between devices: 184 us -> 131 us
  loops' own time: 48.5 us -> 0 us
  between operations: 16 us -> 2.01 us
    pallas_call x0 -> x15, Pallas kernels: none -> 363 us  [call(): pl.pallas_call(kernel, out_shape=outs, in_specs=[spec(small) for small in...]
    psum x1 -> x0, blocking collectives: 199 us -> none  [per_device(): gain_total, table_total = lax.psum((gain_acc, table_acc), ('section', 'dp'))]
    reduce_scatter x1 -> x0, waiting for transfers between devices: 167 us -> none  [per_device(): lax.psum_scatter(for_sending(lax.switch(section, [branch_self, branch_enc...]
    another operation x93 -> x0, local copies, waits for them, and re-layouts: 150 us -> none
    reshape x5 -> x3, local copies, waits for them, and re-layouts: 131 us -> 0.71 us  [the longest x1 0.61 us: per_device(): gains_grad = small[:cut].reshape(gains.shape)]
    dot_general x29 -> x1, matrix products: 123 us -> 1.43 us  [per_device(): jnp.dot(diag[:, :own_buckets.shape[0]], onehot, precision=lax.Precision.H...]
    cond x116 -> x0, local copies, waits for them, and re-layouts: 117 us -> none
    ppermute x13 -> x39, waiting for transfers between devices: 17.7 us -> 131 us  [the longest x15 96.6 us: along_dp(): return lax.ppermute(value, ('section', 'dp'), pairs)]
  transfers between devices with their start and end apart: 14 -> 39, of which waited for: 3 -> 12; matrix products, arithmetic and copies ran while one was open for 43% -> 4% of each run, Pallas kernels for 0% -> 36%
where the time goes in v1:
time: 621 us; the launch traced here: 612 us
  Pallas kernels  363 us (58%)
  waiting for transfers between devices  131 us (21%)
  starting transfers between devices  75.7 us (12%)
  other arithmetic  20 us (3%)
  local copies, waits for them, and re-layouts  18.1 us (3%)
    pallas_call x15, Pallas kernels, call(): pl.pallas_call(kernel, out_shape=outs, in_specs=[spec(small) for small in...  363 us
    ppermute x15, waiting for transfers between devices, along_dp(): return lax.ppermute(value, ('section', 'dp'), pairs)  96.6 us
    ppermute x15, starting transfers between devices, along_dp(): return lax.ppermute(value, ('section', 'dp'), pairs)  37.8 us
    ppermute x19, starting transfers between devices, per_device(): move = lambda value, pairs: lax.ppermute(value, 'section', pairs)  29.1 us
    ppermute x19, waiting for transfers between devices, per_device(): move = lambda value, pairs: lax.ppermute(value, 'section', pairs)  28.3 us
  transfers between devices with their start and end apart: 39, of which 12 were waited for; matrix products, arithmetic and copies ran while one was open for 4% of the time, Pallas kernels for 36%

profile of v1, /device:TPU:2, one launch (start us, length us, event | category | flops | bytes accessed | tf_op | source)
XLA Modules:
  0.0 611.7 jit_solution(10583639189249043576)
XLA Ops:
  0.7 11.0 %slice_bitcast_fusion = (bf16[768,3072]{1,0:T(8,128)(2,1)}, bf16[768,3072]{1,0:T(8,128)(2,1)}, bf16[768,3072]{1,0:T(8,128)(2,1)}) fusion(bf16[1,3,768,3072]{3,2,1,0:T(8,128)(2,1)} %param.9), kind=kLoop, calls=%fused_computation.4 | loop fusion | bytes 28311552 | tf_op jit(solution)/shard_map/squeeze | solution.py:879
  11.6 1.3 collective-permute-start.5
  12.9 1.3 collective-permute-start.6
  14.2 1.3 collective-permute-start.7
  16.7 17.3 %shard_map.94 = (bf16[512,768]{1,0:T(8,128)(2,1)}, bf16[512,768]{1,0:T(8,128)(2,1)}, bf16[512,2304]{1,0:T(8,128)(2,1)}, bf16[512,768]{1,0:T(8,128)(2,1)}, f32[16,512]{1,0:T(8,128)}) custom-call(bf16[1024,768]{1,0:T(8,128)(2,1)} %bitcast.38, bf16[3,768,3072]{2,1,0:T(8,128)(2,1)} %bitcast.28, f32[7,768]{1,0:T(8,128)} %gain_r.19, ...), custom_call_target="tpu_custom_call" | custom-call | flops 7247757312 | bytes 12582912 | tf_op jit(solution)/shard_map/pallas_call | solution.py:236
  34.1 1.5 collective-permute-start
  35.6 17.3 %shard_map.93 = (bf16[512,768]{1,0:T(8,128)(2,1)}, bf16[512,768]{1,0:T(8,128)(2,1)}, bf16[512,2304]{1,0:T(8,128)(2,1)}, bf16[512,768]{1,0:T(8,128)(2,1)}, f32[16,512]{1,0:T(8,128)}) custom-call(bf16[1024,768]{1,0:T(8,128)(2,1)} %bitcast.39, bf16[3,768,3072]{2,1,0:T(8,128)(2,1)} %bitcast.29, f32[7,768]{1,0:T(8,128)} %gain_r.19, ...), custom_call_target="tpu_custom_call" | custom-call | flops 7247757312 | bytes 12582912 | tf_op jit(solution)/shard_map/pallas_call | solution.py:236
  53.7 1.3 collective-permute-start.4
  57.9 1.3 collective-permute-start.3
  59.2 27.9 %collective-permute-done.3.m2_h = bf16[512,768]{1,0:T(8,128)(2,1)S(1)} collective-permute-done((bf16[512,768]{1,0:T(8,128)(2,1)}, bf16[512,768]{1,0:T(8,128)(2,1)S(1)}, u32[]{:S(2)}, u32[]{:S(2)}) %collective-permute-start.3) | collective-permute-done | bytes 786464 | tf_op jit(solution)/shard_map/ppermute | solution.py:877
  87.2 0.9 copy-done.21
  88.0 43.3 %shard_map.97 = (f32[512,768]{1,0:T(8,128)}, f32[512,768]{1,0:T(8,128)}, bf16[512,2304]{1,0:T(8,128)(2,1)}, bf16[512,768]{1,0:T(8,128)(2,1)}, f32[16,512]{1,0:T(...) custom-call(bf16[512,768]{1,0:T(8,128)(2,1)} %get-tuple-element.72.d, ...), custom_call_target="tpu_custom_call" | custom-call | flops 16911433728 | bytes 31457280 | tf_op jit(solution)/shard_map/pallas_call | solution.py:236
  131.3 97.5 %shard_map.98 = (bf16[512,768]{1,0:T(8,128)(2,1)}, bf16[512,768]{1,0:T(8,128)(2,1)}, bf16[512,1536]{1,0:T(8,128)(2,1)}, bf16[512,1536]{1,0:T(8,128)(2,1)}, bf16[...) custom-call(bf16[512,768]{1,0:T(8,128)(2,1)} %get-tuple-element.72.d2_h, ...), custom_call_target="tpu_custom_call" | custom-call | flops 12079595520 | bytes 16777216 | tf_op jit(solution)/shard_map/pallas_call | solution.py:236
  230.4 1.3 collective-permute-start.10
  231.7 1.3 collective-permute-start.12
  233.0 0.9 copy-done.8
  233.9 1.0 shard_map.99
  234.9 1.6 collective-permute-start.9
  236.5 3.9 collective-permute-start.26
  240.4 1.9 collective-permute-start.20
  242.4 2.4 collective-permute-start.21
  247.1 73.7 %shard_map.100 = (f32[512,768]{1,0:T(8,128)}, f32[1,768]{1,0:T(1,128)}, f32[16,1024]{1,0:T(8,128)}, bf16[512,1536]{1,0:T(8,128)(2,1)}, bf16[512,3072]{1,0:T(8,128)(2,1)}) custom-call(bf16[1024,768]{1,0:T(8,128)(2,1)} %bitcast.43, bf16[3,768,3072]{2,1,0:T(8,128)(2,1)} %bitcast.36, f32[7,768]{1,0:T(8,128)} %gain_r.19, f32[2,512]{1,0:T(2,128)} %convert_element_type.120.seg_r, ...), custom_call_target="tpu_custom_call" | custom-call | flops 14495514624 | bytes 16777216 | tf_op jit(solution)/shard_map/pallas_call | solution.py:236
  320.8 2.6 collective-permute-start.13
  323.4 0.9 copy-done.22
  324.3 73.9 %shard_map.102 = (f32[512,768]{1,0:T(8,128)}, f32[1,768]{1,0:T(1,128)}, f32[16,1024]{1,0:T(8,128)}, bf16[512,1536]{1,0:T(8,128)(2,1)}, bf16[512,3072]{1,0:T(8,128)(2,1)}) custom-call(bf16[1024,768]{1,0:T(8,128)(2,1)} %bitcast.44, bf16[3,768,3072]{2,1,0:T(8,128)(2,1)} %bitcast.37, f32[7,768]{1,0:T(8,128)} %gain_r.19, f32[2,512]{1,0:T(2,128)} %convert_element_type.120.seg_r, ...), custom_call_target="tpu_custom_call" | custom-call | flops 14495514624 | bytes 16777216 | tf_op jit(solution)/shard_map/pallas_call | solution.py:236
  398.2 1.4 fusion.6
  400.6 3.0 collective-permute-start.34
  403.6 1.8 collective-permute-done.34
  405.4 2.1 collective-permute-start.35
  407.6 1.7 collective-permute-done.35
  409.4 3.0 collective-permute-start.36
  412.5 1.7 collective-permute-done.36
  414.2 1.9 collective-permute-start.25
  417.5 8.4 %shard_map.105 = (bf16[4,96,1536]{2,1,0:T(8,128)(2,1)}, bf16[4,96,1536]{2,1,0:T(8,128)(2,1)}) custom-call(bf16[512,1536]{1,0:T(8,128)(2,1)} %get-tuple-element.114.args_0_, bf16[512,1536]{1,0:T(8,128)(2,1)} %collective-permute-done.20.args_1_, bf16[512,1536]{1,0:T(8,128)(2,1)} %get-tuple-element.116.args_2_, bf16[512,1536]{1,0:T(8,128)(2,1)} %collective-permute-done.21.args_3_), custom_call_target="tpu_custom_call" | custom-call | flops 2415919104 | bytes 14680064 | tf_op jit(solution)/shard_map/pallas_call | solution.py:236
  426.0 3.8 collective-permute-start.22
  429.9 2.5 select_select_fusion.1
  432.3 1.3 collective-permute-done.38
  433.7 2.1 collective-permute-start.31
  435.8 1.9 maximum_bitcast_fusion.1
  437.6 14.0 %shard_map.103 = (bf16[4,96,3072]{2,1,0:T(8,128)(2,1)}, bf16[4,96,3072]{2,1,0:T(8,128)(2,1)}) custom-call(bf16[512,1536]{1,0:T(8,128)(2,1)} %get-tuple-element.102.args_0_, bf16[512,1536]{1,0:T(8,128)(2,1)} %get-tuple-element.103.args_1_, bf16[512,3072]{1,0:T(8,128)(2,1)} %get-tuple-element.104.args_2_, bf16[512,3072]{1,0:T(8,128)(2,1)} %get-tuple-element.105.args_3_), custom_call_target="tpu_custom_call" | custom-call | flops 4831838208 | bytes 14680064 | tf_op jit(solution)/shard_map/pallas_call | solution.py:236
  453.0 2.1 collective-permute-start.14
  455.1 14.1 %shard_map.106 = (bf16[4,96,3072]{2,1,0:T(8,128)(2,1)}, bf16[4,96,3072]{2,1,0:T(8,128)(2,1)}) custom-call(bf16[512,768]{1,0:T(8,128)(2,1)} %get-tuple-element.120.args_0_, bf16[512,768]{1,0:T(8,128)(2,1)} %collective-permute-done.25.args_1_, bf16[512,3072]{1,0:T(8,128)(2,1)} %get-tuple-element.122.args_2_, bf16[512,3072]{1,0:T(8,128)(2,1)} %collective-permute-done.26.args_3_), custom_call_target="tpu_custom_call" | custom-call | flops 4831838208 | bytes 14680064 | tf_op jit(solution)/shard_map/pallas_call | solution.py:236
  469.2 3.8 collective-permute-start.27
  473.0 1.7 add_convert_fusion.6
  474.8 3.5 collective-permute-start.23
  478.3 0.9 add_convert_fusion.2
  479.3 0.9 collective-permute-start.18
  480.8 2.6 add_convert_fusion
  483.5 0.9 collective-permute-start.32
  484.4 3.5 collective-permute-done.23
  488.0 3.5 collective-permute-start.24
  491.5 43.0 %collective-permute-done.27 = bf16[4,96,3072]{2,1,0:T(8,128)(2,1)S(1)} collective-permute-done((bf16[4,96,3072]{2,1,0:T(8,128)(2,1)}, bf16[4,96,3072]{2,1,0:T(8,128)(2,1)S(1)}, u32[]{:S(2)}, u32[]{:S(2)}) %collective-permute-start.27) | collective-permute-done | bytes 2359328 | tf_op jit(solution)/shard_map/ppermute | solution.py:851
  534.5 0.9 add_convert_fusion.1
  535.5 3.5 collective-permute-start.28
  540.4 18.3 %collective-permute-done.28 = bf16[2,96,3072]{2,1,0:T(8,128)(2,1)S(1)} collective-permute-done((bf16[2,96,3072]{2,1,0:T(8,128)(2,1)S(1)}, bf16[2,96,3072]{2,1,0:T(8,128)(2,1)S(1)}, u32[]{:S(2)}, u32[]{:S(2)}) %collective-permute-start.28) | collective-permute-done | bytes 1179680 | tf_op jit(solution)/shard_map/ppermute | solution.py:851
  559.2 4.4 collective-permute-start.29
  563.6 2.6 add_convert_fusion.3
  566.3 4.4 collective-permute-start.15
  570.7 7.6 %collective-permute-done.29 = bf16[1,96,3072]{2,1,0:T(8,128)(2,1)S(1)} collective-permute-done((bf16[1,96,3072]{2,1,0:T(8,128)(2,1)S(1)}, bf16[1,96,3072]{2,1,0:T(8,128)(2,1)S(1)}, u32[]{:S(2)}, u32[]{:S(2)}) %collective-permute-start.29) | collective-permute-done | bytes 589856 | tf_op jit(solution)/shard_map/ppermute | solution.py:851
  578.7 1.3 collective-permute-start.30
  581.3 8.5 %collective-permute-done.15 = bf16[2,96,3072]{2,1,0:T(8,128)(2,1)S(1)} collective-permute-done((bf16[2,96,3072]{2,1,0:T(8,128)(2,1)S(1)}, bf16[2,96,3072]{2,1,0:T(8,128)(2,1)S(1)}, u32[]{:S(2)}, u32[]{:S(2)}) %collective-permute-start.15) | collective-permute-done | bytes 1179680 | tf_op jit(solution)/shard_map/ppermute | solution.py:851
  590.2 2.7 collective-permute-start.16
  593.3 15.7 %collective-permute-done.16 = bf16[1,96,3072]{2,1,0:T(8,128)(2,1)S(1)} collective-permute-done((bf16[1,96,3072]{2,1,0:T(8,128)(2,1)S(1)}, bf16[1,96,3072]{2,1,0:T(8,128)(2,1)S(1)}, u32[]{:S(2)}, u32[]{:S(2)}) %collective-permute-start.16) | collective-permute-done | bytes 589856 | tf_op jit(solution)/shard_map/ppermute | solution.py:851
  609.5 2.0 maximum_bitcast_fusion
  (135 shorter events, 18.3 us)
Async XLA Ops:
  0.6 14.9 %copy-start.15 = (s32[2,512]{1,0:T(2,128)S(1)}, s32[2,512]{1,0:T(2,128)}, u32[]{:S(2)}) copy-start(s32[2,512]{1,0:T(2,128)} %param.7) | copy-start | bytes 12292
  0.6 15.5 %copy-start.11 = (f32[2,32,12]{1,0,2:T(2,128)S(1)}, f32[2,32,12]{1,0,2:T(2,128)}, u32[]{:S(2)}) copy-start(f32[2,32,12]{1,0,2:T(2,128)} %param.11) | copy-start | bytes 9220
  11.6 75.5 %collective-permute-start.5 = (bf16[768,3072]{1,0:T(8,128)(2,1)}, bf16[768,3072]{1,0:T(8,128)(2,1)}, u32[]{:S(2)}, u32[]{:S(2)}) collective-permute-start(bf16[768,3072]{1,0:T(8,128)(2,1)} %get-tuple-element.145), channel_id=1, source_target_pairs={{24,16},{25,17},{26,18},{27,19},{28,20},{29,21},{30,22},{31,23}} | collective-permute-start | bytes 14155784 | tf_op jit(solution)/shard_map/ppermute | solution.py:877
  12.9 74.2 %collective-permute-start.6 = (bf16[768,3072]{1,0:T(8,128)(2,1)}, bf16[768,3072]{1,0:T(8,128)(2,1)}, u32[]{:S(2)}, u32[]{:S(2)}) collective-permute-start(bf16[768,3072]{1,0:T(8,128)(2,1)} %get-tuple-element.146), channel_id=1, source_target_pairs={{24,16},{25,17},{26,18},{27,19},{28,20},{29,21},{30,22},{31,23}} | collective-permute-start | bytes 14155784 | tf_op jit(solution)/shard_map/ppermute | solution.py:877
  14.2 72.9 %collective-permute-start.7 = (bf16[768,3072]{1,0:T(8,128)(2,1)}, bf16[768,3072]{1,0:T(8,128)(2,1)}, u32[]{:S(2)}, u32[]{:S(2)}) collective-permute-start(bf16[768,3072]{1,0:T(8,128)(2,1)} %get-tuple-element.144), channel_id=1, source_target_pairs={{24,16},{25,17},{26,18},{27,19},{28,20},{29,21},{30,22},{31,23}} | collective-permute-start | bytes 14155784 | tf_op jit(solution)/shard_map/ppermute | solution.py:877
  34.1 19.5 %copy-start = (bf16[1,1024,768]{2,1,0:T(8,128)(2,1)S(1)}, bf16[1,1024,768]{2,1,0:T(8,128)(2,1)}, u32[]{:S(2)}) copy-start(bf16[1,1024,768]{2,1,0:T(8,128)(2,1)} %param.6) | copy-start | bytes 4718596
  34.1 19.6 %collective-permute-start = (bf16[512,768]{1,0:T(8,128)(2,1)}, bf16[512,768]{1,0:T(8,128)(2,1)S(1)}, u32[]{:S(2)}, u32[]{:S(2)}) collective-permute-start(bf16[512,768]{1,0:T(8,128)(2,1)} %get-tuple-element.73), channel_id=1, source_target_pairs={{0,8},{16,24},{1,9},{17,25},{2,10},{18,26},{3,11},{19,27},{4,12},{... | collective-permute-start | bytes 2359304 | tf_op jit(solution)/shard_map/ppermute | solution.py:877
  52.9 3.0 collective-permute-start.2
  53.7 1.3 copy-start.7
  53.7 4.2 collective-permute-start.4
  55.8 0.9 copy-start.6
  55.9 3.3 collective-permute-start.1
  57.9 29.3 %copy-start.19 = (bf16[512,768]{1,0:T(8,128)(2,1)}, bf16[512,768]{1,0:T(8,128)(2,1)S(1)}, u32[]{:S(2)}) copy-start(bf16[512,768]{1,0:T(8,128)(2,1)S(1)} %collective-permute-done.4.c2_h) | copy-start | bytes 2359300
  57.9 29.2 %collective-permute-start.3 = (bf16[512,768]{1,0:T(8,128)(2,1)}, bf16[512,768]{1,0:T(8,128)(2,1)S(1)}, u32[]{:S(2)}, u32[]{:S(2)}) collective-permute-start(bf16[512,768]{1,0:T(8,128)(2,1)} %get-tuple-element.75), channel_id=1, source_target_pairs={{8,16},{9,17},{10,18},{11,19},{12,20},{13,21},{14,22},{15,23}} | collective-permute-start | bytes 2359304 | tf_op jit(solution)/shard_map/ppermute | solution.py:877
  59.2 28.0 %copy-start.20 = (bf16[512,768]{1,0:T(8,128)(2,1)}, bf16[512,768]{1,0:T(8,128)(2,1)S(1)}, u32[]{:S(2)}) copy-start(bf16[512,768]{1,0:T(8,128)(2,1)S(1)} %collective-permute-done.1.m3_h) | copy-start | bytes 2359300
  87.1 0.9 copy-start.21
  131.3 98.2 %copy-start.12 = (s32[2,1023]{1,0:T(2,128)S(1)}, s32[2,1023]{1,0:T(2,128)}, u32[]{:S(2)}) copy-start(s32[2,1023]{1,0:T(2,128)} %bucket_r.3) | copy-start | bytes 24556
  131.3 101.7 %copy-start.13 = (f32[2,768]{1,0:T(2,128)S(1)}, f32[2,768]{1,0:T(2,128)}, u32[]{:S(2)}) copy-start(f32[2,768]{1,0:T(2,128)} %get-tuple-element.137) | copy-start | bytes 18436
  228.8 4.3 collective-permute-start.8
  230.3 4.5 copy-start.10
  230.4 12.0 %collective-permute-start.10 = (bf16[512,768]{1,0:T(8,128)(2,1)}, bf16[512,768]{1,0:T(8,128)(2,1)S(1)}, u32[]{:S(2)}, u32[]{:S(2)}) collective-permute-start(bf16[512,768]{1,0:T(8,128)(2,1)} %get-tuple-element.81), channel_id=1, source_target_pairs={{16,8},{17,9},{18,10},{19,11},{20,12},{21,13},{22,14},{23,15}} | collective-permute-start | bytes 2359304 | tf_op jit(solution)/shard_map/ppermute | solution.py:877
  231.7 89.1 %collective-permute-start.12 = (bf16[512,768]{1,0:T(8,128)(2,1)}, bf16[512,768]{1,0:T(8,128)(2,1)}, u32[]{:S(2)}, u32[]{:S(2)}) collective-permute-start(bf16[512,768]{1,0:T(8,128)(2,1)} %get-tuple-element.85.gd_h), channel_id=1, source_target_pairs={{24,16},{25,17},{26,18},{27,19},{28,20},{29,21},{30,22},{31,23}} | collective-permute-start | bytes 2359304 | tf_op jit(solution)/shard_map/ppermute | solution.py:877
  233.0 0.9 copy-start.8
  233.9 2.6 copy-start.17
  233.9 6.5 %copy-start.18 = (bf16[512,1536]{1,0:T(8,128)(2,1)S(1)}, bf16[512,1536]{1,0:T(8,128)(2,1)}, u32[]{:S(2)}) copy-start(bf16[512,1536]{1,0:T(8,128)(2,1)} %get-tuple-element.115) | copy-start | bytes 4718596
  234.9 11.5 %collective-permute-start.9 = (bf16[512,768]{1,0:T(8,128)(2,1)}, bf16[512,768]{1,0:T(8,128)(2,1)}, u32[]{:S(2)}, u32[]{:S(2)}) collective-permute-start(bf16[512,768]{1,0:T(8,128)(2,1)} %get-tuple-element.84), channel_id=1, source_target_pairs={{8,0},{9,1},{10,2},{11,3},{12,4},{13,5},{14,6},{15,7}} | collective-permute-start | bytes 2359304 | tf_op jit(solution)/shard_map/ppermute | solution.py:877
  236.5 218.6 %collective-permute-start.26 = (bf16[512,3072]{1,0:T(8,128)(2,1)}, bf16[512,3072]{1,0:T(8,128)(2,1)}, u32[]{:S(2)}, u32[]{:S(2)}) collective-permute-start(bf16[512,3072]{1,0:T(8,128)(2,1)} %get-tuple-element.123), channel_id=1, source_target_pairs={{16,24},{24,16},{17,25},{25,17},{18,26},{26,18},{19,27},{27,19},{2... | collective-permute-start | bytes 9437192 | tf_op jit(solution)/shard_map/ppermute | solution.py:877
  240.4 175.7 %collective-permute-start.20 = (bf16[512,1536]{1,0:T(8,128)(2,1)S(1)}, bf16[512,1536]{1,0:T(8,128)(2,1)}, u32[]{:S(2)}, u32[]{:S(2)}) collective-permute-start(bf16[512,1536]{1,0:T(8,128)(2,1)S(1)} %copy-done.18), channel_id=1, source_target_pairs={{16,24},{24,16},{17,25},{25,17},{18,26},{26,18},{19,27},{27,19},{2... | collective-permute-start | bytes 4718600 | tf_op jit(solution)/shard_map/ppermute | solution.py:877
  242.4 2.4 copy-start.9
  242.4 174.6 %collective-permute-start.21 = (bf16[512,1536]{1,0:T(8,128)(2,1)}, bf16[512,1536]{1,0:T(8,128)(2,1)}, u32[]{:S(2)}, u32[]{:S(2)}) collective-permute-start(bf16[512,1536]{1,0:T(8,128)(2,1)} %get-tuple-element.117), channel_id=1, source_target_pairs={{16,24},{24,16},{17,25},{25,17},{18,26},{26,18},{19,27},{27,19},{2... | collective-permute-start | bytes 4718600 | tf_op jit(solution)/shard_map/ppermute | solution.py:877
  244.8 0.9 copy-start.14
  246.4 77.0 %collective-permute-start.11 = (bf16[512,768]{1,0:T(8,128)(2,1)}, bf16[512,768]{1,0:T(8,128)(2,1)S(1)}, u32[]{:S(2)}, u32[]{:S(2)}) collective-permute-start(bf16[512,768]{1,0:T(8,128)(2,1)} %get-tuple-element.98), channel_id=1, source_target_pairs={{8,0},{9,1},{10,2},{11,3},{12,4},{13,5},{14,6},{15,7}} | collective-permute-start | bytes 2359304 | tf_op jit(solution)/shard_map/ppermute | solution.py:877
  320.8 77.4 %copy-start.23 = (f32[16,1024]{1,0:T(8,128)S(1)}, f32[16,1024]{1,0:T(8,128)}, u32[]{:S(2)}) copy-start(f32[16,1024]{1,0:T(8,128)} %get-tuple-element.138) | copy-start | bytes 196612
  320.8 78.9 %copy-start.16 = (f32[1,768]{1,0:T(1,128)S(1)}, f32[1,768]{1,0:T(1,128)}, u32[]{:S(2)}) copy-start(f32[1,768]{1,0:T(1,128)} %get-tuple-element.132) | copy-start | bytes 9220
  320.8 109.0 %collective-permute-start.13 = (f32[512,768]{1,0:T(8,128)}, f32[512,768]{1,0:T(8,128)}, u32[]{:S(2)}, u32[]{:S(2)}) collective-permute-start(f32[512,768]{1,0:T(8,128)} %get-tuple-element.100), channel_id=1, source_target_pairs={{16,24},{17,25},{18,26},{19,27},{20,28},{21,29},{22,30},{23,31}} | collective-permute-start | bytes 4718600 | tf_op jit(solution)/shard_map/ppermute | solution.py:877
  323.4 0.9 copy-start.22
  400.6 4.8 collective-permute-start.34
  405.4 3.9 collective-permute-start.35
  409.4 4.8 collective-permute-start.36
  414.2 38.8 %collective-permute-start.25 = (bf16[512,768]{1,0:T(8,128)(2,1)}, bf16[512,768]{1,0:T(8,128)(2,1)}, u32[]{:S(2)}, u32[]{:S(2)}) collective-permute-start(bf16[512,768]{1,0:T(8,128)(2,1)} %get-tuple-element.121), channel_id=1, source_target_pairs={{16,24},{24,16},{17,25},{25,17},{18,26},{26,18},{19,27},{27,19},{2... | collective-permute-start | bytes 2359304 | tf_op jit(solution)/shard_map/ppermute | solution.py:877
  416.1 62.1 %collective-permute-start.17 = (bf16[4,96,3072]{2,1,0:T(8,128)(2,1)}, bf16[4,96,3072]{2,1,0:T(8,128)(2,1)S(1)}, u32[]{:S(2)}, u32[]{:S(2)}) collective-permute-start(bf16[4,96,3072]{2,1,0:T(8,128)(2,1)} %get-tuple-element.113), channel_id=1, source_target_pairs={{8,9},{9,8},{10,11},{11,10},{12,13},{13,12},{14,15},{15,14}} | collective-permute-start | bytes 7077896 | tf_op jit(solution)/shard_map/ppermute | solution.py:851
  417.0 9.0 %collective-permute-start.37 = (f32[48,128]{1,0:T(8,128)S(1)}, f32[48,128]{1,0:T(8,128)S(1)}, u32[]{:S(2)}, u32[]{:S(2)}) collective-permute-start(f32[48,128]{1,0:T(8,128)S(1)} %add.101), channel_id=1, source_target_pairs={{0,8},{1,9},{2,10},{3,11},{4,12},{5,13},{6,14},{7,15},{8,0},{9,1},... | collective-permute-start | bytes 73736 | tf_op jit(solution)/shard_map/ppermute | solution.py:965
  426.0 47.0 %collective-permute-start.22 = (bf16[4,96,1536]{2,1,0:T(8,128)(2,1)}, bf16[4,96,1536]{2,1,0:T(8,128)(2,1)}, u32[]{:S(2)}, u32[]{:S(2)}) collective-permute-start(bf16[4,96,1536]{2,1,0:T(8,128)(2,1)} %get-tuple-element.119), channel_id=1, source_target_pairs={{16,17},{17,16},{18,19},{19,18},{20,21},{21,20},{22,23},{23,22},{2... | collective-permute-start | bytes 3538952 | tf_op jit(solution)/shard_map/ppermute | solution.py:851
  429.8 3.9 collective-permute-start.38
  433.7 46.5 %collective-permute-start.31 = (bf16[4,96,3072]{2,1,0:T(8,128)(2,1)}, bf16[4,96,3072]{2,1,0:T(8,128)(2,1)}, u32[]{:S(2)}, u32[]{:S(2)}) collective-permute-start(bf16[4,96,3072]{2,1,0:T(8,128)(2,1)} %get-tuple-element.131), channel_id=1, source_target_pairs={{8,9},{9,8},{10,11},{11,10},{12,13},{13,12},{14,15},{15,14}} | collective-permute-start | bytes 7077896 | tf_op jit(solution)/shard_map/ppermute | solution.py:851
  453.0 110.6 %collective-permute-start.14 = (bf16[4,96,3072]{2,1,0:T(8,128)(2,1)}, bf16[4,96,3072]{2,1,0:T(8,128)(2,1)}, u32[]{:S(2)}, u32[]{:S(2)}) collective-permute-start(bf16[4,96,3072]{2,1,0:T(8,128)(2,1)} %get-tuple-element.107), channel_id=1, source_target_pairs={{0,1},{1,0},{2,3},{3,2},{4,5},{5,4},{6,7},{7,6},{16,17},{17,16},{1... | collective-permute-start | bytes 7077896 | tf_op jit(solution)/shard_map/ppermute | solution.py:851
  455.1 17.9 %copy-start.5 = (bf16[4,96,1536]{2,1,0:T(8,128)(2,1)S(1)}, bf16[4,96,1536]{2,1,0:T(8,128)(2,1)}, u32[]{:S(2)}) copy-start(bf16[4,96,1536]{2,1,0:T(8,128)(2,1)} %get-tuple-element.118) | copy-start | bytes 3538948
  469.2 65.3 %collective-permute-start.27 = (bf16[4,96,3072]{2,1,0:T(8,128)(2,1)}, bf16[4,96,3072]{2,1,0:T(8,128)(2,1)S(1)}, u32[]{:S(2)}, u32[]{:S(2)}) collective-permute-start(bf16[4,96,3072]{2,1,0:T(8,128)(2,1)} %get-tuple-element.125), channel_id=1, source_target_pairs={{16,17},{17,16},{18,19},{19,18},{20,21},{21,20},{22,23},{23,22},{2... | collective-permute-start | bytes 7077896 | tf_op jit(solution)/shard_map/ppermute | solution.py:851
  473.0 5.3 copy-start.1
  474.8 13.1 %collective-permute-start.23 = (bf16[2,96,1536]{2,1,0:T(8,128)(2,1)S(1)}, bf16[2,96,1536]{2,1,0:T(8,128)(2,1)S(1)}, u32[]{:S(2)}, u32[]{:S(2)}) collective-permute-start(bf16[2,96,1536]{2,1,0:T(8,128)(2,1)S(1)} %slice.154), channel_id=1, source_target_pairs={{16,18},{17,19},{18,16},{19,17},{20,22},{21,23},{22,20},{23,21},{2... | collective-permute-start | bytes 1769480 | tf_op jit(solution)/shard_map/ppermute | solution.py:851
  479.2 1.7 copy-start.2
  479.3 100.8 %collective-permute-start.18 = (bf16[2,96,3072]{2,1,0:T(8,128)(2,1)S(1)}, bf16[2,96,3072]{2,1,0:T(8,128)(2,1)S(1)}, u32[]{:S(2)}, u32[]{:S(2)}) collective-permute-start(bf16[2,96,3072]{2,1,0:T(8,128)(2,1)S(1)} %slice.150), channel_id=1, source_target_pairs={{8,10},{9,11},{10,8},{11,9},{12,14},{13,15},{14,12},{15,13}} | collective-permute-start | bytes 3538952 | tf_op jit(solution)/shard_map/ppermute | solution.py:851
  483.5 51.0 %copy-start.4 = (bf16[4,96,3072]{2,1,0:T(8,128)(2,1)S(1)}, bf16[4,96,3072]{2,1,0:T(8,128)(2,1)}, u32[]{:S(2)}) copy-start(bf16[4,96,3072]{2,1,0:T(8,128)(2,1)} %get-tuple-element.124) | copy-start | bytes 7077892
  483.5 55.6 %collective-permute-start.32 = (bf16[2,96,3072]{2,1,0:T(8,128)(2,1)S(1)}, bf16[2,96,3072]{2,1,0:T(8,128)(2,1)S(1)}, u32[]{:S(2)}, u32[]{:S(2)}) collective-permute-start(bf16[2,96,3072]{2,1,0:T(8,128)(2,1)S(1)} %slice.163), channel_id=1, source_target_pairs={{8,10},{9,11},{10,8},{11,9},{12,14},{13,15},{14,12},{15,13}} | collective-permute-start | bytes 3538952 | tf_op jit(solution)/shard_map/ppermute | solution.py:851
  488.0 51.0 %collective-permute-start.24 = (bf16[1,96,1536]{2,1,0:T(8,128)(2,1)S(1)}, bf16[1,96,1536]{2,1,0:T(8,128)(2,1)S(1)}, u32[]{:S(2)}, u32[]{:S(2)}) collective-permute-start(bf16[1,96,1536]{2,1,0:T(8,128)(2,1)S(1)} %slice.156), channel_id=1, source_target_pairs={{16,20},{17,21},{18,22},{19,23},{20,16},{21,17},{22,18},{23,19},{2... | collective-permute-start | bytes 884744 | tf_op jit(solution)/shard_map/ppermute | solution.py:851
  535.5 23.2 %collective-permute-start.28 = (bf16[2,96,3072]{2,1,0:T(8,128)(2,1)S(1)}, bf16[2,96,3072]{2,1,0:T(8,128)(2,1)S(1)}, u32[]{:S(2)}, u32[]{:S(2)}) collective-permute-start(bf16[2,96,3072]{2,1,0:T(8,128)(2,1)S(1)} %slice.158), channel_id=1, source_target_pairs={{16,18},{17,19},{18,16},{19,17},{20,22},{21,23},{22,20},{23,21},{2... | collective-permute-start | bytes 3538952 | tf_op jit(solution)/shard_map/ppermute | solution.py:851
  539.6 24.0 %copy-start.3 = (bf16[4,96,3072]{2,1,0:T(8,128)(2,1)S(1)}, bf16[4,96,3072]{2,1,0:T(8,128)(2,1)}, u32[]{:S(2)}) copy-start(bf16[4,96,3072]{2,1,0:T(8,128)(2,1)} %get-tuple-element.106) | copy-start | bytes 7077892
  539.6 31.1 %collective-permute-start.33 = (bf16[1,96,3072]{2,1,0:T(8,128)(2,1)S(1)}, bf16[1,96,3072]{2,1,0:T(8,128)(2,1)S(1)}, u32[]{:S(2)}, u32[]{:S(2)}) collective-permute-start(bf16[1,96,3072]{2,1,0:T(8,128)(2,1)S(1)} %slice.165), channel_id=1, source_target_pairs={{8,12},{9,13},{10,14},{11,15},{12,8},{13,9},{14,10},{15,11}} | collective-permute-start | bytes 1769480 | tf_op jit(solution)/shard_map/ppermute | solution.py:851
  559.2 19.1 %collective-permute-start.29 = (bf16[1,96,3072]{2,1,0:T(8,128)(2,1)S(1)}, bf16[1,96,3072]{2,1,0:T(8,128)(2,1)S(1)}, u32[]{:S(2)}, u32[]{:S(2)}) collective-permute-start(bf16[1,96,3072]{2,1,0:T(8,128)(2,1)S(1)} %slice.160), channel_id=1, source_target_pairs={{16,20},{17,21},{18,22},{19,23},{20,16},{21,17},{22,18},{23,19},{2... | collective-permute-start | bytes 1769480 | tf_op jit(solution)/shard_map/ppermute | solution.py:851
  566.3 23.5 %collective-permute-start.15 = (bf16[2,96,3072]{2,1,0:T(8,128)(2,1)S(1)}, bf16[2,96,3072]{2,1,0:T(8,128)(2,1)S(1)}, u32[]{:S(2)}, u32[]{:S(2)}) collective-permute-start(bf16[2,96,3072]{2,1,0:T(8,128)(2,1)S(1)} %slice.146), channel_id=1, source_target_pairs={{0,2},{1,3},{2,0},{3,1},{4,6},{5,7},{6,4},{7,5},{16,18},{17,19},{1... | collective-permute-start | bytes 3538952 | tf_op jit(solution)/shard_map/ppermute | solution.py:851
  578.7 14.2 %collective-permute-start.30 = (bf16[96,4608]{1,0:T(8,128)(2,1)S(1)}, bf16[96,4608]{1,0:T(8,128)(2,1)S(1)}, u32[]{:S(2)}, u32[]{:S(2)}) collective-permute-start(bf16[96,4608]{1,0:T(8,128)(2,1)S(1)} %pad_maximum_fusion), channel_id=1, source_target_pairs={{16,24},{17,25},{18,26},{19,27},{20,28},{21,29},{22,30},{23,31}} | collective-permute-start | bytes 2654216 | tf_op jit(solution)/shard_map/ppermute | solution.py:877
  580.6 12.8 %collective-permute-start.19 = (bf16[1,96,3072]{2,1,0:T(8,128)(2,1)S(1)}, bf16[1,96,3072]{2,1,0:T(8,128)(2,1)S(1)}, u32[]{:S(2)}, u32[]{:S(2)}) collective-permute-start(bf16[1,96,3072]{2,1,0:T(8,128)(2,1)S(1)} %slice.152), channel_id=1, source_target_pairs={{8,12},{9,13},{10,14},{11,15},{12,8},{13,9},{14,10},{15,11}} | collective-permute-start | bytes 1769480 | tf_op jit(solution)/shard_map/ppermute | solution.py:851
  590.2 18.8 %collective-permute-start.16 = (bf16[1,96,3072]{2,1,0:T(8,128)(2,1)S(1)}, bf16[1,96,3072]{2,1,0:T(8,128)(2,1)S(1)}, u32[]{:S(2)}, u32[]{:S(2)}) collective-permute-start(bf16[1,96,3072]{2,1,0:T(8,128)(2,1)S(1)} %slice.148), channel_id=1, source_target_pairs={{0,4},{1,5},{2,6},{3,7},{4,0},{5,1},{6,2},{7,3},{16,20},{17,21},{1... | collective-permute-start | bytes 1769480 | tf_op jit(solution)/shard_map/ppermute | solution.py:851
